TPU v7x, 256 devices: a whole 4x4x8 slice. The times are simulated.
256 devices in a mesh: dp: 128 (over z, y_hi, x, core), mp: 2 (over y_lo).
Axes of the slice: x: 4, y: 4 (y_hi: 2, y_lo: 2; y = y_hi * 2 + y_lo), z: 8, core: 2. Of those that a mesh axis runs over, the one named last changes fastest.
Arguments:
- img_emb: bfloat16 [16384, 1152], P(('dp', 'mp')), may hold values from -6 to 6
- txt_emb: bfloat16 [16384, 1152], P('dp'), may hold values from -6 to 6
- logit_scale: float32 [1], replicated, may hold values from 5 to 15
- logit_bias: float32 [1], replicated, may hold values from -2.5 to -0.5
- pos_step: int32 [16384], P(('dp', 'mp')), may hold values from 0 to 7
- pos_row: int32 [16384], P(('dp', 'mp')), may hold values from 0 to 127
- acts: bfloat16 [49152, 1152], P('dp'), may hold values from -6 to 6
- cotangent: bfloat16 [49152, 1152], P('dp'), may hold values from -24 to 24
- w_up: bfloat16 [1152, 2304], P(None, 'mp'), may hold values from -0.1875 to 0.1875
- w_down: bfloat16 [1152, 2304], P(None, 'mp'), may hold values from -0.125 to 0.125
Outputs:
- grad_img: float32 [16384, 1152], P(('dp', 'mp'))
- grad_txt: float32 [16384, 1152], P('dp')
- grad_up: float32 [1152, 2304], P('dp', 'mp')
- grad_down: float32 [1152, 2304], P('dp', 'mp')
- grad_acts: bfloat16 [49152, 1152], P('dp')
All inputs are finite; a program needn't handle non-finite values.
Results may differ from a plain program's by a relative error of at most 0.0054.
Values may be sent and summed in bfloat16 or wider, within the bound.
A program may use at most 128 MiB of HBM per device.

v0:
```python
from functools import partial

import jax
import jax.numpy as jnp
from jax import lax
from jax.sharding import PartitionSpec as P

STEPS = 8


def shifted(value, axis, steps):
    count = lax.axis_size(axis)
    pairs = [(source, (source + steps) % count) for source in range(count)]
    return lax.ppermute(value, axis, pairs)


def unit_rows(values):
    full = values.astype(jnp.float32)
    norms = jnp.sqrt(jnp.sum(full * full, axis=-1, keepdims=True) + 1e-06)
    return (full / norms, norms)


def back_unit(unit, norms, grads):
    return (grads - unit * jnp.sum(unit * grads, axis=-1, keepdims=True)) / norms


def loss_grads(img_emb, txt_emb, logit_scale, logit_bias, pos_step, pos_row):
    scale = logit_scale[0]
    bias = logit_bias[0]
    img_unit, img_norm = unit_rows(img_emb)
    txt_unit, txt_norm = unit_rows(txt_emb)
    img_bf = img_unit.astype(jnp.bfloat16)
    txt_bf = txt_unit.astype(jnp.bfloat16)
    block_rows = txt_bf.shape[0]
    col_ids = jnp.arange(block_rows, dtype=jnp.int32)
    own_target = pos_step * block_rows + pos_row

    def meeting(images, target, texts, step):
        logits = (
            scale
            * lax.dot_general(
                images, texts, (((1,), (1,)), ((), ())), preferred_element_type=jnp.float32
            )
            + bias
        )
        positive = target[:, None] == (step * block_rows + col_ids)[None, :]
        label = jnp.where(positive, 1.0, -1.0).astype(jnp.float32)
        dlogit = (-label * jax.nn.sigmoid(-label * logits)).astype(jnp.bfloat16)
        img_part = jnp.dot(dlogit, texts, preferred_element_type=jnp.float32)
        txt_part = lax.dot_general(
            dlogit, images, (((0,), (0,)), ((), ())), preferred_element_type=jnp.float32
        )
        return (img_part, txt_part)

    texts = txt_bf
    img_acc, carried = meeting(img_bf, own_target, texts, 0)
    for step in range(1, STEPS):
        texts = shifted(texts, "dp", 1)
        carried = shifted(carried, "dp", 1)
        img_part, txt_part = meeting(img_bf, own_target, texts, step)
        img_acc = img_acc + img_part
        carried = carried + txt_part
    txt_acc = shifted(carried, "dp", 1 - STEPS)
    txt_total = lax.psum(txt_acc, "mp")
    grad_img = back_unit(img_unit, img_norm, scale * img_acc)
    grad_txt = back_unit(txt_unit, txt_norm, scale * txt_total)
    return (grad_img, grad_txt)


def layer_grads(acts, cotangent, w_up, w_down):
    gelu_fn = partial(jax.nn.gelu, approximate=True)
    full = acts.astype(jnp.float32)
    mean = jnp.mean(full, axis=-1, keepdims=True)
    centred = full - mean
    rstd = lax.rsqrt(jnp.mean(centred * centred, axis=-1, keepdims=True) + 1e-06)
    normed = centred * rstd
    normed_bf = normed.astype(jnp.bfloat16)
    pre = jnp.dot(normed_bf, w_up, preferred_element_type=jnp.float32)
    hidden_f, gelu_back = jax.vjp(gelu_fn, pre)
    hidden = hidden_f.astype(jnp.bfloat16)
    dhidden = jnp.dot(cotangent, w_down, preferred_element_type=jnp.float32)
    dpre = gelu_back(dhidden)[0].astype(jnp.bfloat16)
    width = w_up.shape[1]
    term_up = lax.dot_general(
        normed_bf, dpre, (((0,), (0,)), ((), ())), preferred_element_type=jnp.float32
    )
    term_down = lax.dot_general(
        cotangent, hidden, (((0,), (0,)), ((), ())), preferred_element_type=jnp.float32
    )
    summed = lax.psum_scatter(
        jnp.concatenate([term_up, term_down], axis=1), "dp", scatter_dimension=0, tiled=True
    )
    dnormed_part = lax.dot_general(
        dpre, w_up, (((1,), (1,)), ((), ())), preferred_element_type=jnp.float32
    )
    dnormed = lax.psum(dnormed_part, "mp")
    inner = (
        dnormed
        - jnp.mean(dnormed, axis=-1, keepdims=True)
        - normed * jnp.mean(dnormed * normed, axis=-1, keepdims=True)
    )
    grad_acts = (cotangent.astype(jnp.float32) + rstd * inner).astype(jnp.bfloat16)
    return (summed[:, :width], summed[:, width:], grad_acts)


def shards(
    img_emb, txt_emb, logit_scale, logit_bias, pos_step, pos_row, acts, cotangent, w_up, w_down
):
    grad_img, grad_txt = loss_grads(img_emb, txt_emb, logit_scale, logit_bias, pos_step, pos_row)
    grad_up, grad_down, grad_acts = layer_grads(acts, cotangent, w_up, w_down)
    return (grad_img, grad_txt, grad_up, grad_down, grad_acts)


def solution(mesh):
    return jax.shard_map(
        shards,
        mesh=mesh,
        in_specs=(
            P(("dp", "mp"), None),
            P("dp", None),
            P(),
            P(),
            P(("dp", "mp")),
            P(("dp", "mp")),
            P("dp", None),
            P("dp", None),
            P(None, "mp"),
            P(None, "mp"),
        ),
        out_specs=(
            P(("dp", "mp"), None),
            P("dp", None),
            P("dp", "mp"),
            P("dp", "mp"),
            P("dp", None),
        ),
        check_vma=False,
    )
```

profile of v0, /device:TPU:1, one launch (start us, length us, event | category | flops | bytes accessed | tf_op | source)
XLA Modules:
  0.0 1517.2 jit_solution(8080936642965227032)
XLA Ops:
  7.2 1.3 fusion.87
  9.7 2.7 collective-permute-start
  15.4 1.2 fusion.75
  18.0 3.2 fusion.125
  21.6 1.5 collective-permute-start.1
  24.9 2.6 collective-permute-start.8
  27.8 2.5 collective-permute-start.2
  30.9 5.4 collective-permute-done.8
  37.0 1.8 collective-permute-done.2
  38.8 1.2 collective-permute-start.3
  40.6 10.9 collective-permute-done.9
  51.6 2.4 collective-permute-done.3
  54.7 12.0 collective-permute-done.10
  66.8 2.4 collective-permute-done.4
  69.9 12.0 collective-permute-done.11
  82.0 2.4 collective-permute-done.5
  85.0 12.0 collective-permute-done.12
  97.2 2.4 collective-permute-done.6
  100.2 12.0 collective-permute-done.13
  112.4 3.3 fusion.18
  115.7 2.7 fusion.126
  118.4 11.2 collective-permute-done.14
  129.9 5.3 fusion.95
  135.3 4.1 convolution_bitcast_fusion
  139.4 8.8 pad_maximum_fusion
  153.0 59.9 %all-reduce.7.cloned.1.call-done = (f32[128,1152]{1,0:T(8,128)}, f32[384,1152]{1,0:T(8,128)}) async-done(((f32[128,1152]{1,0:T(8,128)}, f32[384,1152]{1,0:T(8,128)}), (f32[128,1152]{1,0:T(8,128)}, f32[384,1152]{1,0:T(8,128)})) %all-reduce.7.cloned.1.call-update) | async-done | bytes 2359312 | tf_op jit(solution)/shard_map/psum | solution.py:64
  212.9 1.4 multiply_reduce_fusion
  214.3 2.1 fusion.122
  217.5 1.6 fusion.10
  219.1 1285.6 %all-reduce.5.cloned.1.call-done = f32[1152,2304]{0,1:T(8,128)} async-done(((f32[1152,2304]{0,1:T(8,128)}), f32[1152,2304]{0,1:T(8,128)}) %all-reduce.5.cloned.1.call-update) | async-done | bytes 10616848
  1504.7 2.8 fusion.123
  1507.6 1.9 copy.17
  (159 shorter events, 17.8 us)
Async XLA Ops:
  7.2 105.2 %copy-start = (bf16[1152,1152]{1,0:T(8,128)(2,1)S(1)}, bf16[1152,1152]{1,0:T(8,128)(2,1)}, u32[]{:S(2)}) copy-start(bf16[1152,1152]{1,0:T(8,128)(2,1)} %param.18) | copy-start | bytes 7962628
  7.2 10.6 copy-start.2
  7.2 205.7 %all-reduce.7.cloned.1.call-start = ((), (), s32[]{:S(2)}) async-start(), calls=%async_computation.1 | async-start | bytes 4718592 | tf_op jit(solution)/shard_map/psum | solution.py:64
  9.7 11.5 copy-start.12
  9.7 11.9 collective-permute-start
  17.5 7.1 collective-permute-start.7
  21.6 6.2 collective-permute-start.1
  24.9 11.3 collective-permute-start.8
  27.8 11.0 collective-permute-start.2
  36.3 15.1 collective-permute-start.9
  38.8 12.8 copy-start.19
  38.8 15.3 %collective-permute-start.3 = (bf16[128,1152]{1,0:T(8,128)(2,1)S(1)}, bf16[128,1152]{1,0:T(8,128)(2,1)S(1)}, u32[]{:S(2)}, u32[]{:S(2)}) collective-permute-start(bf16[128,1152]{1,0:T(8,128)(2,1)S(1)} %collective-permute-done.2), channel_id=1, source_target_pairs={{0,2},{2,4},{4,6},{6,8},{8,10},{10,12},{12,14},{14,16},{16,18},{18... | collective-permute-start | bytes 884744 | tf_op jit(solution)/shard_map/ppermute | solution.py:14
  40.3 14.1 copy-start.31
  51.5 15.1 collective-permute-start.10
  54.0 12.7 copy-start.21
  54.0 15.2 %collective-permute-start.4 = (bf16[128,1152]{1,0:T(8,128)(2,1)S(1)}, bf16[128,1152]{1,0:T(8,128)(2,1)S(1)}, u32[]{:S(2)}, u32[]{:S(2)}) collective-permute-start(bf16[128,1152]{1,0:T(8,128)(2,1)S(1)} %collective-permute-done.3), channel_id=1, source_target_pairs={{0,2},{2,4},{4,6},{6,8},{8,10},{10,12},{12,14},{14,16},{16,18},{18... | collective-permute-start | bytes 884744 | tf_op jit(solution)/shard_map/ppermute | solution.py:14
  54.4 15.2 %copy-start.33 = (bf16[64,128]{1,0:T(8,128)(2,1)}, bf16[64,128]{1,0:T(8,128)(2,1)S(1)}, u32[]{:S(2)}) copy-start(bf16[64,128]{1,0:T(8,128)(2,1)S(1)} %fusion.79) | copy-start | bytes 49156
  66.7 15.1 collective-permute-start.11
  69.2 12.7 copy-start.23
  69.2 15.2 %collective-permute-start.5 = (bf16[128,1152]{1,0:T(8,128)(2,1)S(1)}, bf16[128,1152]{1,0:T(8,128)(2,1)S(1)}, u32[]{:S(2)}, u32[]{:S(2)}) collective-permute-start(bf16[128,1152]{1,0:T(8,128)(2,1)S(1)} %collective-permute-done.4), channel_id=1, source_target_pairs={{0,2},{2,4},{4,6},{6,8},{8,10},{10,12},{12,14},{14,16},{16,18},{18... | collective-permute-start | bytes 884744 | tf_op jit(solution)/shard_map/ppermute | solution.py:14
  69.5 15.2 %copy-start.35 = (bf16[64,128]{1,0:T(8,128)(2,1)}, bf16[64,128]{1,0:T(8,128)(2,1)S(1)}, u32[]{:S(2)}) copy-start(bf16[64,128]{1,0:T(8,128)(2,1)S(1)} %fusion.80) | copy-start | bytes 49156
  81.9 15.1 collective-permute-start.12
  84.4 12.7 copy-start.25
  84.4 15.2 %collective-permute-start.6 = (bf16[128,1152]{1,0:T(8,128)(2,1)S(1)}, bf16[128,1152]{1,0:T(8,128)(2,1)S(1)}, u32[]{:S(2)}, u32[]{:S(2)}) collective-permute-start(bf16[128,1152]{1,0:T(8,128)(2,1)S(1)} %collective-permute-done.5), channel_id=1, source_target_pairs={{0,2},{2,4},{4,6},{6,8},{8,10},{10,12},{12,14},{14,16},{16,18},{18... | collective-permute-start | bytes 884744 | tf_op jit(solution)/shard_map/ppermute | solution.py:14
  84.7 15.2 copy-start.37
  97.1 15.1 collective-permute-start.13
  99.6 12.7 copy-start.41
  99.9 12.4 copy-start.44
  112.3 17.3 %collective-permute-start.14 = (f32[128,1152]{1,0:T(8,128)S(1)}, f32[128,1152]{1,0:T(8,128)}, u32[]{:S(2)}, u32[]{:S(2)}) collective-permute-start(f32[128,1152]{1,0:T(8,128)S(1)} %add.271), channel_id=1, source_target_pairs={{0,242},{2,244},{4,246},{6,248},{8,250},{10,252},{12,254},{14,0},{... | collective-permute-start | bytes 1769480 | tf_op jit(solution)/shard_map/ppermute | solution.py:14
  129.6 1375.1 %all-reduce.5.cloned.1.call-start = ((), (), s32[]{:S(2)}) async-start(), calls=%async_computation | async-start | bytes 21233664
  151.6 61.4 %copy-start.4 = (bf16[128,1152]{1,0:T(8,128)(2,1)S(1)}, bf16[128,1152]{1,0:T(8,128)(2,1)}, u32[]{:S(2)}) copy-start(bf16[128,1152]{1,0:T(8,128)(2,1)} %param.11) | copy-start | bytes 884740
  217.5 1292.8 %copy-start.1 = (bf16[1152,1152]{1,0:T(8,128)(2,1)S(1)}, bf16[1152,1152]{1,0:T(8,128)(2,1)}, u32[]{:S(2)}) copy-start(bf16[1152,1152]{1,0:T(8,128)(2,1)} %param.18) | copy-start | bytes 7962628
  (31 other events, 108.2 us)
Sparse Core Ops, SparseCore 0:
  129.7 83.1 all-reduce.6
  215.8 1288.9 all-reduce.4
where the time goes:
time: 1520 us
  waiting for transfers between devices  1430 us (94%)
  matrix products  26 us (2%)
  other arithmetic  20.9 us (1%)
  between operations  16.8 us (1%)
    unnamed x3, waiting for transfers between devices  1290 us
    ppermute x15, waiting for transfers between devices, shifted(): return lax.ppermute(value, axis, pairs)  88.1 us
    psum x1, waiting for transfers between devices, loss_grads(): txt_total = lax.psum(txt_acc, 'mp')  59.9 us
  transfers between devices with their start and end apart: 17, of which 16 were waited for; matrix products, arithmetic and copies ran while one was open for 3% of the time, Pallas kernels for 0%

commit v1 on v0

v1 whole, which is shorter than its diff:
```python
import jax
import jax.numpy as jnp
from jax import lax
from jax.experimental import pallas as pl
from jax.experimental.pallas import tpu as pltpu
from jax.sharding import PartitionSpec as P

D = 1152
STEPS = 8
IMGS = 64
TXTS = 128
TOK = 384
HALF = 1152
NZ = 8
ZROWS = D // NZ
SUB = 48
NSUB = ZROWS // SUB
WIN = 32
OUT = 9
META = 128
EPS = 1e-06
MESH = pl.DeviceIdType.MESH
F32 = jnp.float32
BF16 = jnp.bfloat16
GELU_C = 0.7978845608028654
GELU_A = 0.044715
TILES = ((0, 256), (256, 256), (512, 256), (768, 256), (1024, 128))


def rows(start, size, align=16):
    return pl.ds(pl.multiple_of(start, align), size)


def nt_dot(a, b):
    return lax.dot_general(a, b, (((1,), (1,)), ((), ())), preferred_element_type=F32)


def tn_dot(a, b):
    return lax.dot_general(a, b, (((0,), (0,)), ((), ())), preferred_element_type=F32)


def nn_dot(a, b):
    return jnp.dot(a, b, preferred_element_type=F32)


def wide_tiles(body):
    @pl.loop(0, 4)
    def _(t):
        body(pl.multiple_of(t * 256, 256), 256)

    body(1024, 128)


def step_kernel(
    scale_ref,
    bias_ref,
    img_h,
    txt_h,
    meta,
    tcol,
    acts_h,
    cot_h,
    wup_h,
    wdn_h,
    gimg,
    gtxt,
    gup,
    gdn,
    gacts,
    img_in,
    txt_in,
    acts,
    cot,
    wup,
    wdn,
    pair_l,
    pair_r,
    left_in,
    right_in,
    normed,
    rstd,
    dnorm,
    grads,
    up_out,
    up_in,
    dn_out,
    dn_in,
    inner_out,
    inner_in,
    zsum,
    zsum_bf,
    win_in,
    fin_out,
    fin_in,
    texts,
    images,
    txt_unit,
    txt_norm,
    img_unit,
    img_norm,
    gt_out,
    gt_in,
    in_sem,
    text_ss,
    text_rs,
    img_ss,
    img_rs,
    pair_ss,
    pair_rs,
    up_ss,
    up_rs,
    dn_ss,
    dn_rs,
    inner_ss,
    inner_rs,
    win_ss,
    win_rs,
    fin_ss,
    fin_rs,
):
    me = lax.axis_index("dp")
    mp = lax.axis_index("mp")
    core = me % 2
    spot = me % 8
    plane = (me // 2) % 8
    zpos = me // 16
    sibling = me + 1 - 2 * core

    def near(shift):
        moved = spot + shift
        crossed = (moved + 8) // 8
        return ((me + shift + 128) % 128, (mp + crossed + 1) % 2)

    def in_plane(turn):
        return ((zpos * 8 + (plane + turn) % 8) * 2 + core, mp)

    special = ((me + 7 * (2 * core - 1) + 128) % 128, (mp + 1) % 2)
    z_up = ((me + 16) % 128, mp)
    z_dn = ((me + 112) % 128, mp)

    loads = [
        pltpu.make_async_copy(source, target, in_sem.at[i])
        for i, (source, target) in enumerate(
            [
                (txt_h, txt_in),
                (img_h, img_in),
                (acts_h, acts),
                (cot_h, cot),
                (wup_h, wup),
                (wdn_h, wdn),
            ]
        )
    ]
    for load in loads:
        load.start()

    barrier = pltpu.get_barrier_semaphore()
    partners = [near(s) for s in (2, 4, 6, -2, -4, -6)]
    partners += [(sibling, mp), special, (me, 1 - mp), z_up, z_dn]
    partners += [in_plane(q) for q in range(1, 8)]
    for partner in partners:
        pl.semaphore_signal(barrier, inc=1, device_id=partner, device_id_type=MESH)

    def send(source, target, send_sem, recv_sem, device):
        copy = pltpu.make_async_remote_copy(
            src_ref=source,
            dst_ref=target,
            send_sem=send_sem,
            recv_sem=recv_sem,
            device_id=device,
            device_id_type=MESH,
        )
        copy.start()
        pending.append(copy)

    def arrived(target, send_sem, recv_sem):
        pltpu.make_async_remote_copy(
            src_ref=target,
            dst_ref=target,
            send_sem=send_sem,
            recv_sem=recv_sem,
            device_id=(sibling, mp),
            device_id_type=MESH,
        ).wait_recv()

    pending = []

    loads[0].wait()

    @pl.loop(0, TXTS // 16)
    def _(i):
        r = rows(i * 16, 16)
        full = txt_in[r, :].astype(F32)
        norm = jnp.sqrt(jnp.sum(full * full, axis=-1, keepdims=True) + EPS)
        unit = full / norm
        txt_unit[r, :] = unit
        txt_norm[r, :] = jnp.broadcast_to(norm, (16, 128))
        texts[0, r, :] = unit.astype(BF16)

    loads[1].wait()

    @pl.loop(0, IMGS // 16)
    def _(i):
        r = rows(i * 16, 16)
        full = img_in[r, :].astype(F32)
        norm = jnp.sqrt(jnp.sum(full * full, axis=-1, keepdims=True) + EPS)
        unit = full / norm
        img_unit[r, :] = unit
        img_norm[r, :] = jnp.broadcast_to(norm, (16, 128))
        images[0, r, 0:D] = unit.astype(BF16)
        images[0, r, D : D + META] = meta[r, :]

    pl.semaphore_wait(barrier, len(partners))

    for i in (1, 2, 3):
        send(texts.at[0], texts.at[2 * i], text_ss.at[i], text_rs.at[i], near(2 * i))
        send(images.at[0], images.at[2 * i], img_ss.at[i], img_rs.at[i], near(-2 * i))
    text_special = (
        (1 - core) * sibling + core * special[0],
        (1 - core) * mp + core * special[1],
    )
    img_special = (
        core * sibling + (1 - core) * special[0],
        core * mp + (1 - core) * special[1],
    )
    send(texts.at[0], texts.at[1 + 6 * core], text_ss.at[0], text_rs.at[0], text_special)
    send(images.at[0], images.at[7 - 6 * core], img_ss.at[0], img_rs.at[0], img_special)

    loads[2].wait()
    loads[3].wait()

    @pl.loop(0, TOK // 16)
    def _(i):
        r = rows(i * 16, 16)
        full = acts[r, :].astype(F32)
        mean = jnp.mean(full, axis=-1, keepdims=True)
        centred = full - mean
        scale = lax.rsqrt(jnp.mean(centred * centred, axis=-1, keepdims=True) + EPS)
        out = centred * scale
        normed[r, :] = out
        rstd[r, :] = jnp.broadcast_to(scale, (16, 128))
        pair_l[core, r, :] = out.astype(BF16)
        pair_l[1 - core, r, :] = cot[r, :]

    send(pair_l.at[1], left_in, pair_ss.at[0], pair_rs.at[0], (sibling, mp))

    loads[4].wait()
    loads[5].wait()

    def hidden_tile(start, width):
        c = pl.ds(start, width)
        pre = nn_dot(pair_l[core, :, :], wup[:, c])
        dhidden = nn_dot(cot[...], wdn[:, c])
        square = pre * pre
        t = jnp.tanh(GELU_C * (pre + GELU_A * (square * pre)))
        half = 0.5 * (1.0 + t)
        slope = half + (0.5 * GELU_C) * pre * (1.0 - t * t) * (1.0 + (3.0 * GELU_A) * square)
        pair_r[1 - core, :, c] = (pre * half).astype(BF16)
        pair_r[core, :, c] = (dhidden * slope).astype(BF16)

    wide_tiles(hidden_tile)
    send(pair_r.at[1], right_in, pair_ss.at[1], pair_rs.at[1], (sibling, mp))

    def dnorm_tile(start, width):
        c = pl.ds(start, width)
        dnorm[:, c] = nt_dot(pair_r[core, :, :], wup[c, :])

    wide_tiles(dnorm_tile)

    @pl.loop(0, TOK // 16)
    def _(i):
        r = rows(i * 16, 16)
        value = dnorm[r, :]
        unit = normed[r, :]
        inner = (
            value
            - jnp.mean(value, axis=-1, keepdims=True)
            - unit * jnp.mean(value * unit, axis=-1, keepdims=True)
        )
        inner_out[r, :] = inner.astype(BF16)

    send(inner_out, inner_in, inner_ss, inner_rs, (me, 1 - mp))

    arrived(left_in, pair_ss.at[0], pair_rs.at[0])
    arrived(right_in, pair_ss.at[1], pair_rs.at[1])

    def grad_tile(start, width):
        c = pl.ds(start, width)
        grads[c, :] = tn_dot(pair_l[0, :, c], pair_r[0, :, :]) + tn_dot(
            left_in[:, c], right_in[...]
        )

    wide_tiles(grad_tile)

    def up_step(s):
        base = ((zpos + 4 - s) % NZ) * ZROWS
        for c in range(NSUB):
            part = pl.ds(c * SUB, SUB)
            value = grads[rows(base + c * SUB, SUB), :]
            if s > 0:
                arrived(up_in.at[s - 1, part], up_ss.at[s - 1, c], up_rs.at[s - 1, c])
                value = value + up_in[s - 1, part, :].astype(F32)
            up_out[s, part, :] = value.astype(BF16)
            send(up_out.at[s, part], up_in.at[s, part], up_ss.at[s, c], up_rs.at[s, c], z_up)

    def dn_step(s):
        base = ((zpos + 5 + s) % NZ) * ZROWS
        for c in range(NSUB):
            part = pl.ds(c * SUB, SUB)
            value = grads[rows(base + c * SUB, SUB), :]
            if s > 0:
                arrived(dn_in.at[s - 1, part], dn_ss.at[s - 1, c], dn_rs.at[s - 1, c])
                value = value + dn_in[s - 1, part, :].astype(F32)
            dn_out[s, part, :] = value.astype(BF16)
            send(dn_out.at[s, part], dn_in.at[s, part], dn_ss.at[s, c], dn_rs.at[s, c], z_dn)

    up_step(0)
    dn_step(0)

    for i in (1, 2, 3):
        arrived(texts.at[2 * i], text_ss.at[i], text_rs.at[i])
        send(
            texts.at[2 * i],
            texts.at[2 * i + 1 - 2 * core],
            text_ss.at[3 + i],
            text_rs.at[3 + i],
            (sibling, mp),
        )
        arrived(images.at[2 * i], img_ss.at[i], img_rs.at[i])
        send(
            images.at[2 * i],
            images.at[2 * i - 1 + 2 * core],
            img_ss.at[3 + i],
            img_rs.at[3 + i],
            (sibling, mp),
        )

    up_step(1)
    dn_step(1)

    arrived(texts.at[7 - 6 * core], text_ss.at[0], text_rs.at[0])
    arrived(images.at[1 + 6 * core], img_ss.at[0], img_rs.at[0])
    for i in (1, 2, 3):
        arrived(texts.at[2 * i - 1 + 2 * core], text_ss.at[3 + i], text_rs.at[3 + i])
        arrived(images.at[2 * i + 1 - 2 * core], img_ss.at[3 + i], img_rs.at[3 + i])

    scale = scale_ref[0]
    bias = bias_ref[0]

    def slope_of(logits, positive):
        label = jnp.where(positive, 1.0, -1.0).astype(F32)
        return (-label * jax.nn.sigmoid(-label * logits)).astype(BF16)

    own_texts = texts[0]
    text_ids = lax.broadcasted_iota(jnp.int32, (TXTS, 128), 0).astype(F32)
    second = (lax.broadcasted_iota(jnp.int32, (TXTS, 128), 1) // IMGS).astype(F32)
    lane_second = lax.broadcasted_iota(jnp.int32, (16, 128), 1) >= IMGS
    dtxt = jnp.zeros((TXTS, D), F32)
    for pair in range(STEPS // 2):
        block = images[2 * pair : 2 * pair + 2, :, 0:D].reshape(2 * IMGS, D)
        logits = scale * nt_dot(own_texts, block) + bias
        first = images[2 * pair, 0:16, D : D + META].astype(F32)
        later = images[2 * pair + 1, 0:16, D : D + META].astype(F32)
        marks = jnp.where(lane_second, later, first)
        target = marks[0:1, :] * float(TXTS) + marks[1:2, :]
        positive = target == (text_ids + (second + float(2 * pair)) * float(TXTS))
        dtxt = dtxt + nn_dot(slope_of(logits, positive), block)
    dtxt = scale * dtxt
    unit = txt_unit[...]
    back = (dtxt - unit * jnp.sum(unit * dtxt, axis=-1, keepdims=True)) / txt_norm[:, 0:1]
    gt_out[...] = back.astype(BF16)
    send(gt_out, gt_in, pair_ss.at[2], pair_rs.at[2], (me, 1 - mp))

    up_step(2)
    dn_step(2)

    own_images = images[0, :, 0:D]
    cols = lax.broadcasted_iota(jnp.int32, (IMGS, TXTS), 1)
    want = tcol[...]
    dimg = jnp.zeros((IMGS, D), F32)
    for k in range(STEPS):
        block = texts[k]
        logits = scale * nt_dot(own_images, block) + bias
        dimg = dimg + nn_dot(slope_of(logits, want == cols + k * TXTS), block)
    dimg = scale * dimg
    unit = img_unit[...]
    gimg[...] = (dimg - unit * jnp.sum(unit * dimg, axis=-1, keepdims=True)) / img_norm[:, 0:1]

    up_step(3)

    arrived(inner_in, inner_ss, inner_rs)

    @pl.loop(0, TOK // 16)
    def _(i):
        r = rows(i * 16, 16)
        both = inner_out[r, :].astype(F32) + inner_in[r, :].astype(F32)
        gacts[r, :] = (cot[r, :].astype(F32) + rstd[r, 0:1] * both).astype(BF16)

    base = zpos * ZROWS
    for c in range(NSUB):
        part = pl.ds(c * SUB, SUB)
        arrived(up_in.at[3, part], up_ss.at[3, c], up_rs.at[3, c])
        arrived(dn_in.at[2, part], dn_ss.at[2, c], dn_rs.at[2, c])
        value = (
            grads[rows(base + c * SUB, SUB), :]
            + up_in[3, part, :].astype(F32)
            + dn_in[2, part, :].astype(F32)
        )
        zsum[part, :] = value
        zsum_bf[part, :] = value.astype(BF16)
    for q in range(1, 8):
        there = (plane + q) % 8
        send(
            zsum_bf.at[rows(there * 16, WIN)],
            win_in.at[q - 1],
            win_ss.at[q - 1],
            win_rs.at[q - 1],
            in_plane(q),
        )

    arrived(gt_in, pair_ss.at[2], pair_rs.at[2])
    gtxt[...] = gt_out[...].astype(F32) + gt_in[...].astype(F32)

    total = zsum[rows(plane * 16, WIN), :]
    for q in range(1, 8):
        arrived(win_in.at[q - 1], win_ss.at[q - 1], win_rs.at[q - 1])
        total = total + win_in[q - 1].astype(F32)
    fin_out[...] = pltpu.roll(total, (2 * WIN - 2 * plane - OUT * (1 - core)) % WIN, 0)[0:16, :]
    send(fin_out, fin_in, fin_ss, fin_rs, (sibling, mp))
    keep = pltpu.roll(total, (2 * WIN - 2 * plane - OUT * core) % WIN, 0)[0:OUT, :]
    arrived(fin_in, fin_ss, fin_rs)
    other = fin_in[0:OUT, :]
    gup[...] = jnp.where(core == 0, keep, other)
    gdn[...] = jnp.where(core == 0, other, keep)

    for copy in pending:
        copy.wait_send()


def shards(
    img_emb, txt_emb, logit_scale, logit_bias, pos_step, pos_row, acts, cotangent, w_up, w_down
):
    marks = jnp.stack([pos_step, pos_row]).astype(BF16)
    meta = jnp.pad(jnp.tile(marks, (1, 2)), ((0, IMGS - 2), (0, 0)))
    tcol = (pos_step * TXTS + pos_row)[:, None]
    vmem = pl.BlockSpec(memory_space=pltpu.VMEM)
    smem = pl.BlockSpec(memory_space=pltpu.SMEM)
    hbm = pl.BlockSpec(memory_space=pl.ANY)
    dma = pltpu.SemaphoreType.DMA
    out = pl.pallas_call(
        step_kernel,
        out_shape=(
            jax.ShapeDtypeStruct((IMGS, D), F32),
            jax.ShapeDtypeStruct((TXTS, D), F32),
            jax.ShapeDtypeStruct((OUT, HALF), F32),
            jax.ShapeDtypeStruct((OUT, HALF), F32),
            jax.ShapeDtypeStruct((TOK, D), BF16),
        ),
        in_specs=[smem, smem, hbm, hbm, vmem, vmem, hbm, hbm, hbm, hbm],
        out_specs=(vmem, vmem, vmem, vmem, vmem),
        scratch_shapes=[
            pltpu.VMEM((IMGS, D), BF16),
            pltpu.VMEM((TXTS, D), BF16),
            pltpu.VMEM((TOK, D), BF16),
            pltpu.VMEM((TOK, D), BF16),
            pltpu.VMEM((D, HALF), BF16),
            pltpu.VMEM((D, HALF), BF16),
            pltpu.VMEM((2, TOK, D), BF16),
            pltpu.VMEM((2, TOK, HALF), BF16),
            pltpu.VMEM((TOK, D), BF16),
            pltpu.VMEM((TOK, HALF), BF16),
            pltpu.VMEM((TOK, D), F32),
            pltpu.VMEM((TOK, 128), F32),
            pltpu.VMEM((TOK, D), F32),
            pltpu.VMEM((D, HALF), F32),
            pltpu.VMEM((4, ZROWS, HALF), BF16),
            pltpu.VMEM((4, ZROWS, HALF), BF16),
            pltpu.VMEM((3, ZROWS, HALF), BF16),
            pltpu.VMEM((3, ZROWS, HALF), BF16),
            pltpu.VMEM((TOK, D), BF16),
            pltpu.VMEM((TOK, D), BF16),
            pltpu.VMEM((ZROWS, HALF), F32),
            pltpu.VMEM((ZROWS, HALF), BF16),
            pltpu.VMEM((7, WIN, HALF), BF16),
            pltpu.VMEM((16, HALF), F32),
            pltpu.VMEM((16, HALF), F32),
            pltpu.VMEM((STEPS, TXTS, D), BF16),
            pltpu.VMEM((STEPS, IMGS, D + META), BF16),
            pltpu.VMEM((TXTS, D), F32),
            pltpu.VMEM((TXTS, 128), F32),
            pltpu.VMEM((IMGS, D), F32),
            pltpu.VMEM((IMGS, 128), F32),
            pltpu.VMEM((TXTS, D), BF16),
            pltpu.VMEM((TXTS, D), BF16),
            dma((6,)),
            dma((7,)),
            dma((7,)),
            dma((7,)),
            dma((7,)),
            dma((3,)),
            dma((3,)),
            dma((4, NSUB)),
            dma((4, NSUB)),
            dma((3, NSUB)),
            dma((3, NSUB)),
            dma,
            dma,
            dma((7,)),
            dma((7,)),
            dma,
            dma,
        ],
        compiler_params=pltpu.CompilerParams(
            collective_id=0, has_side_effects=True, vmem_limit_bytes=58 * 1024 * 1024
        ),
        name="step",
    )(logit_scale, logit_bias, img_emb, txt_emb, meta, tcol, acts, cotangent, w_up, w_down)
    return out


def solution(mesh):
    return jax.shard_map(
        shards,
        mesh=mesh,
        in_specs=(
            P(("dp", "mp"), None),
            P("dp", None),
            P(),
            P(),
            P(("dp", "mp")),
            P(("dp", "mp")),
            P("dp", None),
            P("dp", None),
            P(None, "mp"),
            P(None, "mp"),
        ),
        out_specs=(
            P(("dp", "mp"), None),
            P("dp", None),
            P("dp", "mp"),
            P("dp", "mp"),
            P("dp", None),
        ),
        check_vma=False,
    )
```

time: 1520 us -> 99.9 us (0.07)
  waiting for transfers between devices: 1430 us -> 0 us
  Pallas kernels: 0 us -> 87.8 us
  matrix products: 26 us -> 0 us
  other arithmetic: 20.9 us -> 0.75 us
    unnamed x3 -> x0, waiting for transfers between devices: 1290 us -> none
    ppermute x15 -> x0, waiting for transfers between devices: 88.1 us -> none  [shifted(): return lax.ppermute(value, axis, pairs)]
    pallas_call x0 -> x1, Pallas kernels: none -> 87.8 us  [shards(): pl.pallas_call(step_kernel, out_shape=(jax.ShapeDtypeStruct((IMGS, D), F3...]
    psum x1 -> x0, waiting for transfers between devices: 59.9 us -> none  [loss_grads(): txt_total = lax.psum(txt_acc, 'mp')]
    dot_general x29 -> x0, matrix products: 26 us -> none  [the longest x1 5.35 us: layer_grads(): lax.dot_general(normed_bf, dpre, (((0,), (0,)), ((), ())), preferred_elem...]
  transfers between devices with their start and end apart: 17 -> 0, of which waited for: 16 -> 0; matrix products, arithmetic and copies ran while one was open for 3% -> 0% of each run, Pallas kernels for 0% -> 0%
where the time goes in v1:
time: 99.9 us; the launch traced here: 99.6 us
  Pallas kernels  87.8 us (88%)
  local copies, waits for them, and re-layouts  9.06 us (9%)
  between operations  1.95 us (2%)
    pallas_call x1, Pallas kernels, shards(): pl.pallas_call(step_kernel, out_shape=(jax.ShapeDtypeStruct((IMGS, D), F3...  87.8 us
    unnamed x7, local copies, waits for them, and re-layouts  7.65 us

profile of v1, /device:TPU:1, one launch (start us, length us, event | category | flops | bytes accessed | tf_op | source)
XLA Modules:
  0.0 99.6 jit_solution(5920722735022174726)
XLA Ops:
  1.9 0.7 add_bitcast_fusion
  2.7 0.1 tile.10
  2.8 0.6 pad.4.meta
  3.4 0.7 copy.15.tcol
  4.1 87.8 %step.1 = (f32[64,1152]{1,0:T(8,128)}, f32[128,1152]{1,0:T(8,128)}, f32[9,1152]{1,0:T(8,128)}, f32[9,1152]{1,0:T(8,128)}, bf16[384,1152]{1,0:T(8,128)(2,1)}) custom-call(f32[1]{0:T(128)S(6)} %copy.21.scale_ref, f32[1]{0:T(128)S(6)} %copy.22.bias_ref, bf16[64,1152]{1,0:T(8,128)(2,1)} %img_h.1, bf16[128,1152]{1,0:T(8,128)(2,1)} %txt_h.1, ...), custom_call_target="tpu_custom_call" | custom-call | tf_op jit(solution)/shard_map/step/pallas_call | solution.py:450
  91.9 0.0 copy-start
  91.9 1.8 %copy.23 = f32[64,1152]{1,0:T(8,128)} copy(f32[64,1152]{1,0:T(8,128)} %get-tuple-element.13) | data formatting | bytes 589824
  93.7 1.9 %copy.24 = f32[128,1152]{1,0:T(8,128)} copy(f32[128,1152]{1,0:T(8,128)} %get-tuple-element.14) | data formatting | bytes 1179648
  95.6 1.5 %copy.25 = f32[9,1152]{1,0:T(8,128)} copy(f32[9,1152]{1,0:T(8,128)} %get-tuple-element.15) | data formatting | bytes 82944
  97.1 1.5 %copy.26 = f32[9,1152]{1,0:T(8,128)} copy(f32[9,1152]{1,0:T(8,128)} %get-tuple-element.16) | data formatting | bytes 82944
  98.6 0.0 copy-done
  98.6 0.9 copy.27
  (2 shorter events, 0.0 us)
Async XLA Ops:
  91.9 6.7 %copy-start = (bf16[384,1152]{1,0:T(8,128)(2,1)S(1)}, bf16[384,1152]{1,0:T(8,128)(2,1)}, u32[]{:S(2)}) copy-start(bf16[384,1152]{1,0:T(8,128)(2,1)} %get-tuple-element.17) | copy-start | bytes 2654212

commit v2 on v1

--- a/solution.py
+++ b/solution.py
@@ -9,6 +9,7 @@
 STEPS = 8
 IMGS = 64
 TXTS = 128
+HTXT = 64
 TOK = 384
 HALF = 1152
 NZ = 8
@@ -18,6 +19,7 @@
 WIN = 32
 OUT = 9
 META = 128
+LN = 64
 EPS = 1e-06
 MESH = pl.DeviceIdType.MESH
 F32 = jnp.float32
@@ -56,8 +58,8 @@
     bias_ref,
     img_h,
     txt_h,
-    meta,
-    tcol,
+    pstep,
+    prow,
     acts_h,
     cot_h,
     wup_h,
@@ -92,14 +94,19 @@
     win_in,
     fin_out,
     fin_in,
+    own_texts,
     texts,
     images,
+    img_too,
+    both,
     txt_unit,
     txt_norm,
     img_unit,
     img_norm,
     gt_out,
     gt_in,
+    gi_out,
+    gi_in,
     in_sem,
     text_ss,
     text_rs,
@@ -143,7 +150,7 @@
         for i, (source, target) in enumerate(
             [
                 (txt_h, txt_in),
-                (img_h, img_in),
+                (img_h, img_in.at[:, pl.ds(0, D)]),
                 (acts_h, acts),
                 (cot_h, cot),
                 (wup_h, wup),
@@ -187,32 +194,59 @@
 
     loads[0].wait()
 
-    @pl.loop(0, TXTS // 16)
+    @pl.loop(0, TXTS // LN)
     def _(i):
-        r = rows(i * 16, 16)
+        r = rows(i * LN, LN)
         full = txt_in[r, :].astype(F32)
         norm = jnp.sqrt(jnp.sum(full * full, axis=-1, keepdims=True) + EPS)
         unit = full / norm
         txt_unit[r, :] = unit
-        txt_norm[r, :] = jnp.broadcast_to(norm, (16, 128))
-        texts[0, r, :] = unit.astype(BF16)
+        txt_norm[r, :] = jnp.broadcast_to(norm, (LN, 128))
+        own_texts[r, :] = unit.astype(BF16)
 
     loads[1].wait()
 
-    @pl.loop(0, IMGS // 16)
+    @pl.loop(0, IMGS // LN)
     def _(i):
-        r = rows(i * 16, 16)
-        full = img_in[r, :].astype(F32)
+        r = rows(i * LN, LN)
+        full = img_in[r, 0:D].astype(F32)
         norm = jnp.sqrt(jnp.sum(full * full, axis=-1, keepdims=True) + EPS)
         unit = full / norm
         img_unit[r, :] = unit
-        img_norm[r, :] = jnp.broadcast_to(norm, (16, 128))
+        img_norm[r, :] = jnp.broadcast_to(norm, (LN, 128))
         images[0, r, 0:D] = unit.astype(BF16)
-        images[0, r, D : D + META] = meta[r, :]
+
+    texts[0] = own_texts[rows(mp * HTXT, HTXT), :]
+
+    mark_row = lax.broadcasted_iota(jnp.int32, (IMGS, IMGS), 0)
+    mark_col = lax.broadcasted_iota(jnp.int32, (IMGS, IMGS), 1)
+    marks = jnp.where(mark_row == 0, pstep[...], prow[...]).astype(F32).astype(BF16)
+    for place in (0, IMGS):
+        images[0, :, D + place : D + place + IMGS] = marks
+        img_in[:, D + place : D + place + IMGS] = marks
+
+    loads[2].wait()
+    loads[3].wait()
+
+    @pl.loop(0, TOK // LN)
+    def _(i):
+        r = rows(i * LN, LN)
+        full = acts[r, :].astype(F32)
+        mean = jnp.mean(full, axis=-1, keepdims=True)
+        centred = full - mean
+        scale = lax.rsqrt(jnp.mean(centred * centred, axis=-1, keepdims=True) + EPS)
+        out = centred * scale
+        normed[r, :] = out
+        rstd[r, :] = jnp.broadcast_to(scale, (LN, 128))
+        pair_l[core, r, :] = out.astype(BF16)
+        pair_l[1 - core, r, :] = cot[r, :]
 
     pl.semaphore_wait(barrier, len(partners))
 
-    for i in (1, 2, 3):
+    send(pair_l.at[1], left_in, pair_ss.at[0], pair_rs.at[0], (sibling, mp))
+
+    send(img_in, img_too, pair_ss.at[3], pair_rs.at[3], (me, 1 - mp))
+    for i in (1, 3, 2):
         send(texts.at[0], texts.at[2 * i], text_ss.at[i], text_rs.at[i], near(2 * i))
         send(images.at[0], images.at[2 * i], img_ss.at[i], img_rs.at[i], near(-2 * i))
     text_special = (
@@ -226,24 +260,6 @@
     send(texts.at[0], texts.at[1 + 6 * core], text_ss.at[0], text_rs.at[0], text_special)
     send(images.at[0], images.at[7 - 6 * core], img_ss.at[0], img_rs.at[0], img_special)
 
-    loads[2].wait()
-    loads[3].wait()
-
-    @pl.loop(0, TOK // 16)
-    def _(i):
-        r = rows(i * 16, 16)
-        full = acts[r, :].astype(F32)
-        mean = jnp.mean(full, axis=-1, keepdims=True)
-        centred = full - mean
-        scale = lax.rsqrt(jnp.mean(centred * centred, axis=-1, keepdims=True) + EPS)
-        out = centred * scale
-        normed[r, :] = out
-        rstd[r, :] = jnp.broadcast_to(scale, (16, 128))
-        pair_l[core, r, :] = out.astype(BF16)
-        pair_l[1 - core, r, :] = cot[r, :]
-
-    send(pair_l.at[1], left_in, pair_ss.at[0], pair_rs.at[0], (sibling, mp))
-
     loads[4].wait()
     loads[5].wait()
 
@@ -261,15 +277,44 @@
     wide_tiles(hidden_tile)
     send(pair_r.at[1], right_in, pair_ss.at[1], pair_rs.at[1], (sibling, mp))
 
+    arrived(left_in, pair_ss.at[0], pair_rs.at[0])
+    arrived(right_in, pair_ss.at[1], pair_rs.at[1])
+
+    def grad_tile(start, width):
+        c = pl.ds(start, width)
+        grads[c, :] = tn_dot(pair_l[0, :, c], pair_r[0, :, :]) + tn_dot(
+            left_in[:, c], right_in[...]
+        )
+
+    wide_tiles(grad_tile)
+
+    def hop(s, c, shift, out, came, ss, rs, device):
+        base = ((zpos + shift) % NZ) * ZROWS
+        part = pl.ds(c * SUB, SUB)
+        value = grads[rows(base + c * SUB, SUB), :]
+        if s > 0:
+            arrived(came.at[s - 1, part], ss.at[s - 1, c], rs.at[s - 1, c])
+            value = value + came[s - 1, part, :].astype(F32)
+        out[s, part, :] = value.astype(BF16)
+        send(out.at[s, part], came.at[s, part], ss.at[s, c], rs.at[s, c], device)
+
+    def z_step(s):
+        for c in range(NSUB):
+            hop(s, c, 4 - s, up_out, up_in, up_ss, up_rs, z_up)
+            if s < 3:
+                hop(s, c, 5 + s, dn_out, dn_in, dn_ss, dn_rs, z_dn)
+
+    z_step(0)
+
     def dnorm_tile(start, width):
         c = pl.ds(start, width)
         dnorm[:, c] = nt_dot(pair_r[core, :, :], wup[c, :])
 
     wide_tiles(dnorm_tile)
 
-    @pl.loop(0, TOK // 16)
+    @pl.loop(0, TOK // LN)
     def _(i):
-        r = rows(i * 16, 16)
+        r = rows(i * LN, LN)
         value = dnorm[r, :]
         unit = normed[r, :]
         inner = (
@@ -281,41 +326,9 @@
 
     send(inner_out, inner_in, inner_ss, inner_rs, (me, 1 - mp))
 
-    arrived(left_in, pair_ss.at[0], pair_rs.at[0])
-    arrived(right_in, pair_ss.at[1], pair_rs.at[1])
-
-    def grad_tile(start, width):
-        c = pl.ds(start, width)
-        grads[c, :] = tn_dot(pair_l[0, :, c], pair_r[0, :, :]) + tn_dot(
-            left_in[:, c], right_in[...]
-        )
-
-    wide_tiles(grad_tile)
-
-    def up_step(s):
-        base = ((zpos + 4 - s) % NZ) * ZROWS
-        for c in range(NSUB):
-            part = pl.ds(c * SUB, SUB)
-            value = grads[rows(base + c * SUB, SUB), :]
-            if s > 0:
-                arrived(up_in.at[s - 1, part], up_ss.at[s - 1, c], up_rs.at[s - 1, c])
-                value = value + up_in[s - 1, part, :].astype(F32)
-            up_out[s, part, :] = value.astype(BF16)
-            send(up_out.at[s, part], up_in.at[s, part], up_ss.at[s, c], up_rs.at[s, c], z_up)
-
-    def dn_step(s):
-        base = ((zpos + 5 + s) % NZ) * ZROWS
-        for c in range(NSUB):
-            part = pl.ds(c * SUB, SUB)
-            value = grads[rows(base + c * SUB, SUB), :]
-            if s > 0:
-                arrived(dn_in.at[s - 1, part], dn_ss.at[s - 1, c], dn_rs.at[s - 1, c])
-                value = value + dn_in[s - 1, part, :].astype(F32)
-            dn_out[s, part, :] = value.astype(BF16)
-            send(dn_out.at[s, part], dn_in.at[s, part], dn_ss.at[s, c], dn_rs.at[s, c], z_dn)
-
-    up_step(0)
-    dn_step(0)
+    z_step(1)
+
+    z_step(2)
 
     for i in (1, 2, 3):
         arrived(texts.at[2 * i], text_ss.at[i], text_rs.at[i])
@@ -335,8 +348,7 @@
             (sibling, mp),
         )
 
-    up_step(1)
-    dn_step(1)
+    z_step(3)
 
     arrived(texts.at[7 - 6 * core], text_ss.at[0], text_rs.at[0])
     arrived(images.at[1 + 6 * core], img_ss.at[0], img_rs.at[0])
@@ -351,50 +363,65 @@
         label = jnp.where(positive, 1.0, -1.0).astype(F32)
         return (-label * jax.nn.sigmoid(-label * logits)).astype(BF16)
 
-    own_texts = texts[0]
+    def target_of(marked):
+        return marked[0:1, :] * float(TXTS) + marked[1:2, :]
+
+    def project(value, unit, norm):
+        return (value - unit * jnp.sum(unit * value, axis=-1, keepdims=True)) / norm
+
+    words = own_texts[...]
     text_ids = lax.broadcasted_iota(jnp.int32, (TXTS, 128), 0).astype(F32)
     second = (lax.broadcasted_iota(jnp.int32, (TXTS, 128), 1) // IMGS).astype(F32)
     lane_second = lax.broadcasted_iota(jnp.int32, (16, 128), 1) >= IMGS
     dtxt = jnp.zeros((TXTS, D), F32)
     for pair in range(STEPS // 2):
         block = images[2 * pair : 2 * pair + 2, :, 0:D].reshape(2 * IMGS, D)
-        logits = scale * nt_dot(own_texts, block) + bias
+        logits = scale * nt_dot(words, block) + bias
         first = images[2 * pair, 0:16, D : D + META].astype(F32)
         later = images[2 * pair + 1, 0:16, D : D + META].astype(F32)
-        marks = jnp.where(lane_second, later, first)
-        target = marks[0:1, :] * float(TXTS) + marks[1:2, :]
+        target = target_of(jnp.where(lane_second, later, first))
         positive = target == (text_ids + (second + float(2 * pair)) * float(TXTS))
         dtxt = dtxt + nn_dot(slope_of(logits, positive), block)
-    dtxt = scale * dtxt
-    unit = txt_unit[...]
-    back = (dtxt - unit * jnp.sum(unit * dtxt, axis=-1, keepdims=True)) / txt_norm[:, 0:1]
-    gt_out[...] = back.astype(BF16)
+    gt_out[...] = project(scale * dtxt, txt_unit[...], txt_norm[:, 0:1]).astype(BF16)
     send(gt_out, gt_in, pair_ss.at[2], pair_rs.at[2], (me, 1 - mp))
 
-    up_step(2)
-    dn_step(2)
-
-    own_images = images[0, :, 0:D]
-    cols = lax.broadcasted_iota(jnp.int32, (IMGS, TXTS), 1)
-    want = tcol[...]
-    dimg = jnp.zeros((IMGS, D), F32)
-    for k in range(STEPS):
-        block = texts[k]
-        logits = scale * nt_dot(own_images, block) + bias
-        dimg = dimg + nn_dot(slope_of(logits, want == cols + k * TXTS), block)
-    dimg = scale * dimg
-    unit = img_unit[...]
-    gimg[...] = (dimg - unit * jnp.sum(unit * dimg, axis=-1, keepdims=True)) / img_norm[:, 0:1]
-
-    up_step(3)
+    arrived(img_too, pair_ss.at[3], pair_rs.at[3])
+    full = img_too[:, 0:D].astype(F32)
+    norm = jnp.sqrt(jnp.sum(full * full, axis=-1, keepdims=True) + EPS)
+    unit = full / norm
+    img_unit[IMGS:, :] = unit
+    img_norm[IMGS:, :] = jnp.broadcast_to(norm, (IMGS, 128))
+    both[0:IMGS, :] = images[0, :, 0:D]
+    both[IMGS:, :] = unit.astype(BF16)
+
+    def as_column(marked):
+        line = target_of(marked.astype(F32))[:, 0:IMGS]
+        return jnp.sum(jnp.where(mark_row == mark_col, line, 0.0), axis=-1, keepdims=True)
+
+    want = jnp.concatenate(
+        [as_column(img_in[0:16, D : D + META]), as_column(img_too[0:16, D : D + META])], axis=0
+    )
+    lane = lax.broadcasted_iota(jnp.int32, (2 * IMGS, 2 * HTXT), 1)
+    pictures = both[...]
+    dimg = jnp.zeros((2 * IMGS, D), F32)
+    for pair in range(STEPS // 2):
+        block = texts[2 * pair : 2 * pair + 2].reshape(2 * HTXT, D)
+        starts = [k * TXTS + near(-k)[1] * HTXT for k in (2 * pair, 2 * pair + 1)]
+        column = jnp.where(lane < HTXT, lane + starts[0], lane + (starts[1] - HTXT))
+        logits = scale * nt_dot(pictures, block) + bias
+        dimg = dimg + nn_dot(slope_of(logits, want == column.astype(F32)), block)
+    dimg = project(scale * dimg, img_unit[...], img_norm[:, 0:1])
+    gimg[...] = dimg[0:IMGS, :]
+    gi_out[...] = dimg[IMGS:, :].astype(BF16)
+    send(gi_out, gi_in, pair_ss.at[4], pair_rs.at[4], (me, 1 - mp))
 
     arrived(inner_in, inner_ss, inner_rs)
 
-    @pl.loop(0, TOK // 16)
+    @pl.loop(0, TOK // LN)
     def _(i):
-        r = rows(i * 16, 16)
-        both = inner_out[r, :].astype(F32) + inner_in[r, :].astype(F32)
-        gacts[r, :] = (cot[r, :].astype(F32) + rstd[r, 0:1] * both).astype(BF16)
+        r = rows(i * LN, LN)
+        total = inner_out[r, :].astype(F32) + inner_in[r, :].astype(F32)
+        gacts[r, :] = (cot[r, :].astype(F32) + rstd[r, 0:1] * total).astype(BF16)
 
     base = zpos * ZROWS
     for c in range(NSUB):
@@ -420,6 +447,8 @@
 
     arrived(gt_in, pair_ss.at[2], pair_rs.at[2])
     gtxt[...] = gt_out[...].astype(F32) + gt_in[...].astype(F32)
+    arrived(gi_in, pair_ss.at[4], pair_rs.at[4])
+    gimg[...] = gimg[...] + gi_in[...].astype(F32)
 
     total = zsum[rows(plane * 16, WIN), :]
     for q in range(1, 8):
@@ -437,12 +466,16 @@
         copy.wait_send()
 
 
+def hand_over(*refs):
+    for i in range(5):
+        refs[5 + i][...] = refs[i][...]
+
+
 def shards(
     img_emb, txt_emb, logit_scale, logit_bias, pos_step, pos_row, acts, cotangent, w_up, w_down
 ):
-    marks = jnp.stack([pos_step, pos_row]).astype(BF16)
-    meta = jnp.pad(jnp.tile(marks, (1, 2)), ((0, IMGS - 2), (0, 0)))
-    tcol = (pos_step * TXTS + pos_row)[:, None]
+    pstep = pos_step.reshape(1, IMGS)
+    prow = pos_row.reshape(1, IMGS)
     vmem = pl.BlockSpec(memory_space=pltpu.VMEM)
     smem = pl.BlockSpec(memory_space=pltpu.SMEM)
     hbm = pl.BlockSpec(memory_space=pl.ANY)
@@ -459,7 +492,7 @@
         in_specs=[smem, smem, hbm, hbm, vmem, vmem, hbm, hbm, hbm, hbm],
         out_specs=(vmem, vmem, vmem, vmem, vmem),
         scratch_shapes=[
-            pltpu.VMEM((IMGS, D), BF16),
+            pltpu.VMEM((IMGS, D + META), BF16),
             pltpu.VMEM((TXTS, D), BF16),
             pltpu.VMEM((TOK, D), BF16),
             pltpu.VMEM((TOK, D), BF16),
@@ -484,21 +517,26 @@
             pltpu.VMEM((7, WIN, HALF), BF16),
             pltpu.VMEM((16, HALF), F32),
             pltpu.VMEM((16, HALF), F32),
-            pltpu.VMEM((STEPS, TXTS, D), BF16),
+            pltpu.VMEM((TXTS, D), BF16),
+            pltpu.VMEM((STEPS, HTXT, D), BF16),
             pltpu.VMEM((STEPS, IMGS, D + META), BF16),
+            pltpu.VMEM((IMGS, D + META), BF16),
+            pltpu.VMEM((2 * IMGS, D), BF16),
             pltpu.VMEM((TXTS, D), F32),
             pltpu.VMEM((TXTS, 128), F32),
-            pltpu.VMEM((IMGS, D), F32),
-            pltpu.VMEM((IMGS, 128), F32),
+            pltpu.VMEM((2 * IMGS, D), F32),
+            pltpu.VMEM((2 * IMGS, 128), F32),
             pltpu.VMEM((TXTS, D), BF16),
             pltpu.VMEM((TXTS, D), BF16),
+            pltpu.VMEM((IMGS, D), BF16),
+            pltpu.VMEM((IMGS, D), BF16),
             dma((6,)),
             dma((7,)),
             dma((7,)),
             dma((7,)),
             dma((7,)),
-            dma((3,)),
-            dma((3,)),
+            dma((5,)),
+            dma((5,)),
             dma((4, NSUB)),
             dma((4, NSUB)),
             dma((3, NSUB)),
@@ -514,8 +552,14 @@
             collective_id=0, has_side_effects=True, vmem_limit_bytes=58 * 1024 * 1024
         ),
         name="step",
-    )(logit_scale, logit_bias, img_emb, txt_emb, meta, tcol, acts, cotangent, w_up, w_down)
-    return out
+    )(logit_scale, logit_bias, img_emb, txt_emb, pstep, prow, acts, cotangent, w_up, w_down)
+    return pl.pallas_call(
+        hand_over,
+        out_shape=tuple(jax.ShapeDtypeStruct(x.shape, x.dtype) for x in out),
+        in_specs=[vmem] * 5,
+        out_specs=(vmem,) * 5,
+        name="hand_over",
+    )(*out)
 
 
 def solution(mesh):

time: 99.9 us -> 73.6 us (0.74)
  Pallas kernels: 87.8 us -> 71.5 us
  local copies, waits for them, and re-layouts: 9.06 us -> 0 us
    pallas_call x1, Pallas kernels: 87.8 us -> 68.7 us  [shards(): pl.pallas_call(step_kernel, out_shape=(jax.ShapeDtypeStruct((IMGS, D), F3...]
    unnamed x7 -> x0, local copies, waits for them, and re-layouts: 7.65 us -> none
    pallas_call x0 -> x1, Pallas kernels: none -> 2.78 us  [shards(): pl.pallas_call(hand_over, out_shape=tuple((jax.ShapeDtypeStruct(x.shape,...]
where the time goes in v2:
time: 73.6 us; the launch traced here: 73.4 us
  Pallas kernels  71.5 us (97%)
  between operations  1.93 us (3%)
    pallas_call x1, Pallas kernels, shards(): pl.pallas_call(step_kernel, out_shape=(jax.ShapeDtypeStruct((IMGS, D), F3...  68.7 us
    pallas_call x1, Pallas kernels, shards(): pl.pallas_call(hand_over, out_shape=tuple((jax.ShapeDtypeStruct(x.shape,...  2.78 us

profile of v2, /device:TPU:1, one launch (start us, length us, event | category | flops | bytes accessed | tf_op | source)
XLA Modules:
  0.0 73.4 jit_solution(106760160565097037)
XLA Ops:
  1.9 68.7 %step.1 = (f32[64,1152]{1,0:T(8,128)}, f32[128,1152]{1,0:T(8,128)}, f32[9,1152]{1,0:T(8,128)}, f32[9,1152]{1,0:T(8,128)}, bf16[384,1152]{1,0:T(8,128)(2,1)}) custom-call(f32[1]{0:T(128)S(6)} %copy.15.scale_ref, f32[1]{0:T(128)S(6)} %copy.16.bias_ref, bf16[64,1152]{1,0:T(8,128)(2,1)} %img_h.1, bf16[128,1152]{1,0:T(8,128)(2,1)} %txt_h.1, s32[1,64]{1,0:T(1,128)} %bitcast.2, ...), custom_call_target="tpu_custom_call" | custom-call | tf_op jit(solution)/shard_map/step/pallas_call | solution.py:483
  70.6 2.8 %hand_over.1 = (f32[64,1152]{1,0:T(8,128)}, f32[128,1152]{1,0:T(8,128)}, f32[9,1152]{1,0:T(8,128)}, f32[9,1152]{1,0:T(8,128)}, bf16[384,1152]{1,0:T(8,128)(2,1)}) custom-call(f32[64,1152]{1,0:T(8,128)} %get-tuple-element.10.refs_0_, f32[128,1152]{1,0:T(8,128)} %get-tuple-element.11.refs_1_, f32[9,1152]{1,0:T(8,128)} %get-tuple-element.12.refs_2_, ...), custom_call_target="tpu_custom_call" | custom-call | tf_op jit(solution)/shard_map/hand_over/pallas_call | solution.py:556

commit v3 on v2

--- a/solution.py
+++ b/solution.py
@@ -16,6 +16,14 @@
 ZROWS = D // NZ
 SUB = 48
 NSUB = ZROWS // SUB
+CZ = 768
+CX = HALF - CZ
+NX = 4
+HWIN = 24
+ZWIN = 2 * HWIN
+XROWS = NZ * ZWIN
+XSUB = 2 * ZWIN
+NXSUB = XROWS // XSUB
 WIN = 32
 OUT = 9
 META = 128
@@ -89,9 +97,18 @@
     dn_in,
     inner_out,
     inner_in,
+    xd_out,
+    xd_in,
+    xu_out,
+    xu_in,
     zsum,
     zsum_bf,
+    xsum,
+    xsum_bf,
     win_in,
+    zwin_in,
+    y_out,
+    y_in,
     fin_out,
     fin_in,
     own_texts,
@@ -120,8 +137,16 @@
     dn_rs,
     inner_ss,
     inner_rs,
+    xd_ss,
+    xd_rs,
+    xu_ss,
+    xu_rs,
     win_ss,
     win_rs,
+    zwin_ss,
+    zwin_rs,
+    y_ss,
+    y_rs,
     fin_ss,
     fin_rs,
 ):
@@ -142,28 +167,33 @@
         return ((zpos * 8 + (plane + turn) % 8) * 2 + core, mp)
 
     special = ((me + 7 * (2 * core - 1) + 128) % 128, (mp + 1) % 2)
-    z_up = ((me + 16) % 128, mp)
-    z_dn = ((me + 112) % 128, mp)
-
-    loads = [
-        pltpu.make_async_copy(source, target, in_sem.at[i])
-        for i, (source, target) in enumerate(
-            [
-                (txt_h, txt_in),
-                (img_h, img_in.at[:, pl.ds(0, D)]),
-                (acts_h, acts),
-                (cot_h, cot),
-                (wup_h, wup),
-                (wdn_h, wdn),
-            ]
-        )
-    ]
-    for load in loads:
-        load.start()
+    xpos = plane % 4
+    half = plane // 4
+    x_up = (me + 2 * ((xpos + 1) % 4 - xpos), mp)
+    x_dn = (me + 2 * ((xpos + 3) % 4 - xpos), mp)
+
+    def along_z(turn):
+        return ((me + 16 * turn) % 128, mp)
+
+    z_up = along_z(1)
+    z_dn = along_z(7)
+
+    def load(source, target, i):
+        copy = pltpu.make_async_copy(source, target, in_sem.at[i])
+        copy.start()
+        return copy
+
+    acts_load = load(acts_h, acts, 0)
+    txt_load = load(txt_h, txt_in, 1)
+    img_load = load(img_h, img_in.at[:, pl.ds(0, D)], 2)
+    wup_load = load(wup_h, wup, 3)
+    cot_load = load(cot_h, cot, 4)
+    wdn_load = load(wdn_h, wdn, 5)
 
     barrier = pltpu.get_barrier_semaphore()
     partners = [near(s) for s in (2, 4, 6, -2, -4, -6)]
-    partners += [(sibling, mp), special, (me, 1 - mp), z_up, z_dn]
+    partners += [(sibling, mp), special, (me, 1 - mp)]
+    partners += [along_z(q) for q in range(1, 8)]
     partners += [in_plane(q) for q in range(1, 8)]
     for partner in partners:
         pl.semaphore_signal(barrier, inc=1, device_id=partner, device_id_type=MESH)
@@ -192,7 +222,7 @@
 
     pending = []
 
-    loads[0].wait()
+    txt_load.wait()
 
     @pl.loop(0, TXTS // LN)
     def _(i):
@@ -204,7 +234,7 @@
         txt_norm[r, :] = jnp.broadcast_to(norm, (LN, 128))
         own_texts[r, :] = unit.astype(BF16)
 
-    loads[1].wait()
+    img_load.wait()
 
     @pl.loop(0, IMGS // LN)
     def _(i):
@@ -225,8 +255,7 @@
         images[0, :, D + place : D + place + IMGS] = marks
         img_in[:, D + place : D + place + IMGS] = marks
 
-    loads[2].wait()
-    loads[3].wait()
+    acts_load.wait()
 
     @pl.loop(0, TOK // LN)
     def _(i):
@@ -239,6 +268,12 @@
         normed[r, :] = out
         rstd[r, :] = jnp.broadcast_to(scale, (LN, 128))
         pair_l[core, r, :] = out.astype(BF16)
+
+    cot_load.wait()
+
+    @pl.loop(0, TOK // LN)
+    def _(i):
+        r = rows(i * LN, LN)
         pair_l[1 - core, r, :] = cot[r, :]
 
     pl.semaphore_wait(barrier, len(partners))
@@ -260,8 +295,8 @@
     send(texts.at[0], texts.at[1 + 6 * core], text_ss.at[0], text_rs.at[0], text_special)
     send(images.at[0], images.at[7 - 6 * core], img_ss.at[0], img_rs.at[0], img_special)
 
-    loads[4].wait()
-    loads[5].wait()
+    wup_load.wait()
+    wdn_load.wait()
 
     def hidden_tile(start, width):
         c = pl.ds(start, width)
@@ -275,36 +310,8 @@
         pair_r[core, :, c] = (dhidden * slope).astype(BF16)
 
     wide_tiles(hidden_tile)
+
     send(pair_r.at[1], right_in, pair_ss.at[1], pair_rs.at[1], (sibling, mp))
-
-    arrived(left_in, pair_ss.at[0], pair_rs.at[0])
-    arrived(right_in, pair_ss.at[1], pair_rs.at[1])
-
-    def grad_tile(start, width):
-        c = pl.ds(start, width)
-        grads[c, :] = tn_dot(pair_l[0, :, c], pair_r[0, :, :]) + tn_dot(
-            left_in[:, c], right_in[...]
-        )
-
-    wide_tiles(grad_tile)
-
-    def hop(s, c, shift, out, came, ss, rs, device):
-        base = ((zpos + shift) % NZ) * ZROWS
-        part = pl.ds(c * SUB, SUB)
-        value = grads[rows(base + c * SUB, SUB), :]
-        if s > 0:
-            arrived(came.at[s - 1, part], ss.at[s - 1, c], rs.at[s - 1, c])
-            value = value + came[s - 1, part, :].astype(F32)
-        out[s, part, :] = value.astype(BF16)
-        send(out.at[s, part], came.at[s, part], ss.at[s, c], rs.at[s, c], device)
-
-    def z_step(s):
-        for c in range(NSUB):
-            hop(s, c, 4 - s, up_out, up_in, up_ss, up_rs, z_up)
-            if s < 3:
-                hop(s, c, 5 + s, dn_out, dn_in, dn_ss, dn_rs, z_dn)
-
-    z_step(0)
 
     def dnorm_tile(start, width):
         c = pl.ds(start, width)
@@ -326,9 +333,66 @@
 
     send(inner_out, inner_in, inner_ss, inner_rs, (me, 1 - mp))
 
-    z_step(1)
-
-    z_step(2)
+    arrived(left_in, pair_ss.at[0], pair_rs.at[0])
+    arrived(right_in, pair_ss.at[1], pair_rs.at[1])
+
+    def grad_tile(start, width):
+        c = pl.ds(start, width)
+        grads[c, :] = tn_dot(pair_l[0, :, c], pair_r[0]) + tn_dot(left_in[:, c], right_in[...])
+
+    wide_tiles(grad_tile)
+
+    def hop(s, c, shift, out, came, ss, rs, device):
+        base = ((zpos + shift) % NZ) * ZROWS
+        part = pl.ds(c * SUB, SUB)
+        value = grads[rows(base + c * SUB, SUB), 0:CZ]
+        if s > 0:
+            arrived(came.at[s - 1, part], ss.at[s - 1, c], rs.at[s - 1, c])
+            value = value + came[s - 1, part, :].astype(F32)
+        out[s, part, :] = value.astype(BF16)
+        send(out.at[s, part], came.at[s, part], ss.at[s, c], rs.at[s, c], device)
+
+    def x_term(shift, c):
+        there = (xpos + shift) % NX
+        return jnp.concatenate(
+            [
+                grads[rows(144 * z + 72 * h + 16 * there, HWIN, 8), CZ:]
+                for z in (2 * c, 2 * c + 1)
+                for h in (0, 1)
+            ],
+            axis=0,
+        )
+
+    def x_hop(s, c, shift, out, came, ss, rs, device, add):
+        part = pl.ds(c * XSUB, XSUB)
+        value = x_term(shift, c)
+        if add:
+            arrived(came.at[0, part], ss.at[0, c], rs.at[0, c])
+            value = value + came[0, part, :].astype(F32)
+        out[s, part, :] = value.astype(BF16)
+        send(out.at[s, part], came.at[s, part], ss.at[s, c], rs.at[s, c], device)
+
+    def x_down(s, c, shift, add=False):
+        x_hop(s, c, shift, xd_out, xd_in, xd_ss, xd_rs, x_dn, add)
+
+    def x_over(s, c, shift, add=False):
+        x_hop(s, c, shift, xu_out, xu_in, xu_ss, xu_rs, x_up, add)
+
+    def z_step(s):
+        for c in range(NSUB):
+            hop(s, c, 4 - s, up_out, up_in, up_ss, up_rs, z_up)
+            if s < 3:
+                hop(s, c, 5 + s, dn_out, dn_in, dn_ss, dn_rs, z_dn)
+
+    z_step(0)
+
+    x_down(0, 0, 2)
+    x_over(0, 2, 2)
+    x_down(0, 1, 2)
+    x_over(0, 3, 2)
+    for c in (2, 3):
+        x_down(1, c, 3)
+        x_over(1, c - 2, 1)
 
     for i in (1, 2, 3):
         arrived(texts.at[2 * i], text_ss.at[i], text_rs.at[i])
@@ -348,7 +412,11 @@
             (sibling, mp),
         )
 
-    z_step(3)
+    z_step(1)
+
+    for c in (0, 1):
+        x_down(1, c, 3, True)
+        x_over(1, c + 2, 1, True)
 
     arrived(texts.at[7 - 6 * core], text_ss.at[0], text_rs.at[0])
     arrived(images.at[1 + 6 * core], img_ss.at[0], img_rs.at[0])
@@ -384,6 +452,8 @@
         dtxt = dtxt + nn_dot(slope_of(logits, positive), block)
     gt_out[...] = project(scale * dtxt, txt_unit[...], txt_norm[:, 0:1]).astype(BF16)
     send(gt_out, gt_in, pair_ss.at[2], pair_rs.at[2], (me, 1 - mp))
+
+    z_step(2)
 
     arrived(img_too, pair_ss.at[3], pair_rs.at[3])
     full = img_too[:, 0:D].astype(F32)
@@ -415,6 +485,25 @@
     gi_out[...] = dimg[IMGS:, :].astype(BF16)
     send(gi_out, gi_in, pair_ss.at[4], pair_rs.at[4], (me, 1 - mp))
 
+    z_step(3)
+
+    for c in range(NXSUB):
+        part = pl.ds(c * XSUB, XSUB)
+        arrived(xd_in.at[1, part], xd_ss.at[1, c], xd_rs.at[1, c])
+        arrived(xu_in.at[1, part], xu_ss.at[1, c], xu_rs.at[1, c])
+        value = x_term(0, c) + xd_in[1, part, :].astype(F32) + xu_in[1, part, :].astype(F32)
+        xsum[part, :] = value
+        xsum_bf[part, :] = value.astype(BF16)
+
+    for q in (4, 3, 5, 2, 6, 1, 7):
+        send(
+            xsum_bf.at[rows((zpos + q) % NZ * ZWIN, ZWIN)],
+            zwin_in.at[q - 1],
+            zwin_ss.at[q - 1],
+            zwin_rs.at[q - 1],
+            along_z(q),
+        )
+
     arrived(inner_in, inner_ss, inner_rs)
 
     @pl.loop(0, TOK // LN)
@@ -429,13 +518,13 @@
         arrived(up_in.at[3, part], up_ss.at[3, c], up_rs.at[3, c])
         arrived(dn_in.at[2, part], dn_ss.at[2, c], dn_rs.at[2, c])
         value = (
-            grads[rows(base + c * SUB, SUB), :]
+            grads[rows(base + c * SUB, SUB), 0:CZ]
             + up_in[3, part, :].astype(F32)
             + dn_in[2, part, :].astype(F32)
         )
         zsum[part, :] = value
         zsum_bf[part, :] = value.astype(BF16)
-    for q in range(1, 8):
+    for q in (6, 5, 4, 3, 2, 7, 1):
         there = (plane + q) % 8
         send(
             zsum_bf.at[rows(there * 16, WIN)],
@@ -445,6 +534,22 @@
             in_plane(q),
         )
 
+    total = xsum[rows(zpos * ZWIN, ZWIN), :]
+    for q in range(1, 8):
+        arrived(zwin_in.at[q - 1], zwin_ss.at[q - 1], zwin_rs.at[q - 1])
+        total = total + zwin_in[q - 1].astype(F32)
+
+    def turned(value, start):
+        size = value.shape[0]
+        return pltpu.roll(value, (size - start) % size, 0)
+
+    lower, upper = total[0:HWIN, :], total[HWIN:, :]
+    y_out[...] = jnp.concatenate(
+        [jnp.where(half == 0, upper, lower), jnp.zeros((WIN - HWIN, CX), F32)], axis=0
+    ).astype(BF16)
+    send(y_out, y_in, y_ss, y_rs, in_plane(4))
+    mine_x = jnp.where(half == 0, lower, upper)
+
     arrived(gt_in, pair_ss.at[2], pair_rs.at[2])
     gtxt[...] = gt_out[...].astype(F32) + gt_in[...].astype(F32)
     arrived(gi_in, pair_ss.at[4], pair_rs.at[4])
@@ -454,9 +559,15 @@
     for q in range(1, 8):
         arrived(win_in.at[q - 1], win_ss.at[q - 1], win_rs.at[q - 1])
         total = total + win_in[q - 1].astype(F32)
-    fin_out[...] = pltpu.roll(total, (2 * WIN - 2 * plane - OUT * (1 - core)) % WIN, 0)[0:16, :]
+    mine_z = turned(total, 2 * plane)
+    arrived(y_in, y_ss, y_rs)
+    mine_x = turned(mine_x + y_in[...].astype(F32)[0:HWIN, :], 2 * xpos)
+    fin_out[:, 0:CZ] = turned(mine_z, OUT * (1 - core))[0:16, :]
+    fin_out[:, CZ:] = turned(mine_x, OUT * (1 - core))[0:16, :]
     send(fin_out, fin_in, fin_ss, fin_rs, (sibling, mp))
-    keep = pltpu.roll(total, (2 * WIN - 2 * plane - OUT * core) % WIN, 0)[0:OUT, :]
+    keep = jnp.concatenate(
+        [turned(mine_z, OUT * core)[0:OUT, :], turned(mine_x, OUT * core)[0:OUT, :]], axis=1
+    )
     arrived(fin_in, fin_ss, fin_rs)
     other = fin_in[0:OUT, :]
     gup[...] = jnp.where(core == 0, keep, other)
@@ -506,15 +617,24 @@
             pltpu.VMEM((TOK, 128), F32),
             pltpu.VMEM((TOK, D), F32),
             pltpu.VMEM((D, HALF), F32),
-            pltpu.VMEM((4, ZROWS, HALF), BF16),
-            pltpu.VMEM((4, ZROWS, HALF), BF16),
-            pltpu.VMEM((3, ZROWS, HALF), BF16),
-            pltpu.VMEM((3, ZROWS, HALF), BF16),
+            pltpu.VMEM((4, ZROWS, CZ), BF16),
+            pltpu.VMEM((4, ZROWS, CZ), BF16),
+            pltpu.VMEM((3, ZROWS, CZ), BF16),
+            pltpu.VMEM((3, ZROWS, CZ), BF16),
             pltpu.VMEM((TOK, D), BF16),
             pltpu.VMEM((TOK, D), BF16),
-            pltpu.VMEM((ZROWS, HALF), F32),
-            pltpu.VMEM((ZROWS, HALF), BF16),
-            pltpu.VMEM((7, WIN, HALF), BF16),
+            pltpu.VMEM((2, XROWS, CX), BF16),
+            pltpu.VMEM((2, XROWS, CX), BF16),
+            pltpu.VMEM((2, XROWS, CX), BF16),
+            pltpu.VMEM((2, XROWS, CX), BF16),
+            pltpu.VMEM((ZROWS, CZ), F32),
+            pltpu.VMEM((ZROWS, CZ), BF16),
+            pltpu.VMEM((XROWS, CX), F32),
+            pltpu.VMEM((XROWS, CX), BF16),
+            pltpu.VMEM((7, WIN, CZ), BF16),
+            pltpu.VMEM((7, ZWIN, CX), BF16),
+            pltpu.VMEM((WIN, CX), BF16),
+            pltpu.VMEM((WIN, CX), BF16),
             pltpu.VMEM((16, HALF), F32),
             pltpu.VMEM((16, HALF), F32),
             pltpu.VMEM((TXTS, D), BF16),
@@ -543,8 +663,16 @@
             dma((3, NSUB)),
             dma,
             dma,
+            dma((2, NXSUB)),
+            dma((2, NXSUB)),
+            dma((2, NXSUB)),
+            dma((2, NXSUB)),
             dma((7,)),
             dma((7,)),
+            dma((7,)),
+            dma((7,)),
+            dma,
+            dma,
             dma,
             dma,
         ],

time: 73.6 us -> 65 us (0.88)
  Pallas kernels: 71.5 us -> 62.9 us
    pallas_call x1, Pallas kernels: 68.7 us -> 60.2 us  [shards(): pl.pallas_call(step_kernel, out_shape=(jax.ShapeDtypeStruct((IMGS, D), F3...]
where the time goes in v3:
time: 65 us; the launch traced here: 64.9 us
  Pallas kernels  62.9 us (97%)
  between operations  1.93 us (3%)
    pallas_call x1, Pallas kernels, shards(): pl.pallas_call(step_kernel, out_shape=(jax.ShapeDtypeStruct((IMGS, D), F3...  60.2 us
    pallas_call x1, Pallas kernels, shards(): pl.pallas_call(hand_over, out_shape=tuple((jax.ShapeDtypeStruct(x.shape,...  2.78 us

profile of v3, /device:TPU:1, one launch (start us, length us, event | category | flops | bytes accessed | tf_op | source)
XLA Modules:
  0.0 64.9 jit_solution(9749623074033673090)
XLA Ops:
  1.9 60.2 %step.1 = (f32[64,1152]{1,0:T(8,128)}, f32[128,1152]{1,0:T(8,128)}, f32[9,1152]{1,0:T(8,128)}, f32[9,1152]{1,0:T(8,128)}, bf16[384,1152]{1,0:T(8,128)(2,1)}) custom-call(f32[1]{0:T(128)S(6)} %copy.15.scale_ref, f32[1]{0:T(128)S(6)} %copy.16.bias_ref, bf16[64,1152]{1,0:T(8,128)(2,1)} %img_h.1, bf16[128,1152]{1,0:T(8,128)(2,1)} %txt_h.1, s32[1,64]{1,0:T(1,128)} %bitcast.2, ...), custom_call_target="tpu_custom_call" | custom-call | tf_op jit(solution)/shard_map/step/pallas_call | solution.py:594
  62.1 2.8 %hand_over.1 = (f32[64,1152]{1,0:T(8,128)}, f32[128,1152]{1,0:T(8,128)}, f32[9,1152]{1,0:T(8,128)}, f32[9,1152]{1,0:T(8,128)}, bf16[384,1152]{1,0:T(8,128)(2,1)}) custom-call(f32[64,1152]{1,0:T(8,128)} %get-tuple-element.10.refs_0_, f32[128,1152]{1,0:T(8,128)} %get-tuple-element.11.refs_1_, f32[9,1152]{1,0:T(8,128)} %get-tuple-element.12.refs_2_, ...), custom_call_target="tpu_custom_call" | custom-call | tf_op jit(solution)/shard_map/hand_over/pallas_call | solution.py:684

commit v4 on v3

--- a/solution.py
+++ b/solution.py
@@ -24,7 +24,6 @@
 XROWS = NZ * ZWIN
 XSUB = 2 * ZWIN
 NXSUB = XROWS // XSUB
-WIN = 32
 OUT = 9
 META = 128
 LN = 64
@@ -72,6 +71,11 @@
     cot_h,
     wup_h,
     wdn_h,
+    gimg_h,
+    gtxt_h,
+    gup_h,
+    gdn_h,
+    gacts_h,
     gimg,
     gtxt,
     gup,
@@ -102,15 +106,14 @@
     xu_out,
     xu_in,
     zsum,
-    zsum_bf,
     xsum,
     xsum_bf,
+    win_out,
     win_in,
     zwin_in,
     y_out,
     y_in,
-    fin_out,
-    fin_in,
+    parts,
     own_texts,
     texts,
     images,
@@ -147,8 +150,6 @@
     zwin_rs,
     y_ss,
     y_rs,
-    fin_ss,
-    fin_rs,
 ):
     me = lax.axis_index("dp")
     mp = lax.axis_index("mp")
@@ -163,8 +164,8 @@
         crossed = (moved + 8) // 8
         return ((me + shift + 128) % 128, (mp + crossed + 1) % 2)
 
-    def in_plane(turn):
-        return ((zpos * 8 + (plane + turn) % 8) * 2 + core, mp)
+    def in_plane(turn, to_core):
+        return ((zpos * 8 + (plane + turn) % 8) * 2 + to_core, mp)
 
     special = ((me + 7 * (2 * core - 1) + 128) % 128, (mp + 1) % 2)
     xpos = plane % 4
@@ -194,7 +195,7 @@
     partners = [near(s) for s in (2, 4, 6, -2, -4, -6)]
     partners += [(sibling, mp), special, (me, 1 - mp)]
     partners += [along_z(q) for q in range(1, 8)]
-    partners += [in_plane(q) for q in range(1, 8)]
+    partners += [in_plane(q, to) for q in range(1, 8) for to in (core, 1 - core)]
     for partner in partners:
         pl.semaphore_signal(barrier, inc=1, device_id=partner, device_id_type=MESH)
 
@@ -281,7 +282,7 @@
     send(pair_l.at[1], left_in, pair_ss.at[0], pair_rs.at[0], (sibling, mp))
 
     send(img_in, img_too, pair_ss.at[3], pair_rs.at[3], (me, 1 - mp))
-    for i in (1, 3, 2):
+    for i in (1, 3):
         send(texts.at[0], texts.at[2 * i], text_ss.at[i], text_rs.at[i], near(2 * i))
         send(images.at[0], images.at[2 * i], img_ss.at[i], img_rs.at[i], near(-2 * i))
     text_special = (
@@ -310,7 +311,6 @@
         pair_r[core, :, c] = (dhidden * slope).astype(BF16)
 
     wide_tiles(hidden_tile)
-
     send(pair_r.at[1], right_in, pair_ss.at[1], pair_rs.at[1], (sibling, mp))
 
     def dnorm_tile(start, width):
@@ -333,6 +333,28 @@
 
     send(inner_out, inner_in, inner_ss, inner_rs, (me, 1 - mp))
 
+    def hand_on(i):
+        send(
+            texts.at[2 * i],
+            texts.at[2 * i + 1 - 2 * core],
+            text_ss.at[3 + i],
+            text_rs.at[3 + i],
+            (sibling, mp),
+        )
+        send(
+            images.at[2 * i],
+            images.at[2 * i - 1 + 2 * core],
+            img_ss.at[3 + i],
+            img_rs.at[3 + i],
+            (sibling, mp),
+        )
+
+    arrived(texts.at[2], text_ss.at[1], text_rs.at[1])
+    send(texts.at[2], texts.at[4], text_ss.at[2], text_rs.at[2], near(2))
+    arrived(images.at[2], img_ss.at[1], img_rs.at[1])
+    send(images.at[2], images.at[4], img_ss.at[2], img_rs.at[2], near(-2))
+    hand_on(1)
+
     arrived(left_in, pair_ss.at[0], pair_rs.at[0])
     arrived(right_in, pair_ss.at[1], pair_rs.at[1])
 
@@ -394,29 +416,18 @@
         x_down(1, c, 3)
         x_over(1, c - 2, 1)
 
-    for i in (1, 2, 3):
-        arrived(texts.at[2 * i], text_ss.at[i], text_rs.at[i])
-        send(
-            texts.at[2 * i],
-            texts.at[2 * i + 1 - 2 * core],
-            text_ss.at[3 + i],
-            text_rs.at[3 + i],
-            (sibling, mp),
-        )
-        arrived(images.at[2 * i], img_ss.at[i], img_rs.at[i])
-        send(
-            images.at[2 * i],
-            images.at[2 * i - 1 + 2 * core],
-            img_ss.at[3 + i],
-            img_rs.at[3 + i],
-            (sibling, mp),
-        )
-
     z_step(1)
 
     for c in (0, 1):
         x_down(1, c, 3, True)
         x_over(1, c + 2, 1, True)
+
+    for i in (3, 2):
+        arrived(texts.at[2 * i], text_ss.at[i], text_rs.at[i])
+        arrived(images.at[2 * i], img_ss.at[i], img_rs.at[i])
+        hand_on(i)
+
+    z_step(2)
 
     arrived(texts.at[7 - 6 * core], text_ss.at[0], text_rs.at[0])
     arrived(images.at[1 + 6 * core], img_ss.at[0], img_rs.at[0])
@@ -453,7 +464,24 @@
     gt_out[...] = project(scale * dtxt, txt_unit[...], txt_norm[:, 0:1]).astype(BF16)
     send(gt_out, gt_in, pair_ss.at[2], pair_rs.at[2], (me, 1 - mp))
 
-    z_step(2)
+    z_step(3)
+
+    for c in range(NXSUB):
+        part = pl.ds(c * XSUB, XSUB)
+        arrived(xd_in.at[1, part], xd_ss.at[1, c], xd_rs.at[1, c])
+        arrived(xu_in.at[1, part], xu_ss.at[1, c], xu_rs.at[1, c])
+        value = x_term(0, c) + xd_in[1, part, :].astype(F32) + xu_in[1, part, :].astype(F32)
+        xsum[part, :] = value
+        xsum_bf[part, :] = value.astype(BF16)
+
+    for q in (4, 3, 5, 2, 6, 1, 7):
+        send(
+            xsum_bf.at[rows((zpos + q) % NZ * ZWIN, ZWIN)],
+            zwin_in.at[q - 1],
+            zwin_ss.at[q - 1],
+            zwin_rs.at[q - 1],
+            along_z(q),
+        )
 
     arrived(img_too, pair_ss.at[3], pair_rs.at[3])
     full = img_too[:, 0:D].astype(F32)
@@ -485,25 +513,6 @@
     gi_out[...] = dimg[IMGS:, :].astype(BF16)
     send(gi_out, gi_in, pair_ss.at[4], pair_rs.at[4], (me, 1 - mp))
 
-    z_step(3)
-
-    for c in range(NXSUB):
-        part = pl.ds(c * XSUB, XSUB)
-        arrived(xd_in.at[1, part], xd_ss.at[1, c], xd_rs.at[1, c])
-        arrived(xu_in.at[1, part], xu_ss.at[1, c], xu_rs.at[1, c])
-        value = x_term(0, c) + xd_in[1, part, :].astype(F32) + xu_in[1, part, :].astype(F32)
-        xsum[part, :] = value
-        xsum_bf[part, :] = value.astype(BF16)
-
-    for q in (4, 3, 5, 2, 6, 1, 7):
-        send(
-            xsum_bf.at[rows((zpos + q) % NZ * ZWIN, ZWIN)],
-            zwin_in.at[q - 1],
-            zwin_ss.at[q - 1],
-            zwin_rs.at[q - 1],
-            along_z(q),
-        )
-
     arrived(inner_in, inner_ss, inner_rs)
 
     @pl.loop(0, TOK // LN)
@@ -511,6 +520,8 @@
         r = rows(i * LN, LN)
         total = inner_out[r, :].astype(F32) + inner_in[r, :].astype(F32)
         gacts[r, :] = (cot[r, :].astype(F32) + rstd[r, 0:1] * total).astype(BF16)
+
+    stores = [load(gacts, gacts_h, 6)]
 
     base = zpos * ZROWS
     for c in range(NSUB):
@@ -523,55 +534,66 @@
             + dn_in[2, part, :].astype(F32)
         )
         zsum[part, :] = value
-        zsum_bf[part, :] = value.astype(BF16)
-    for q in (6, 5, 4, 3, 2, 7, 1):
-        there = (plane + q) % 8
-        send(
-            zsum_bf.at[rows(there * 16, WIN)],
-            win_in.at[q - 1],
-            win_ss.at[q - 1],
-            win_rs.at[q - 1],
-            in_plane(q),
-        )
+    zsum[ZROWS:, :] = jnp.zeros((16, CZ), F32)
+    for there in range(8):
+        for to in range(2):
+            first = 2 * OUT * there + OUT * to
+            win_out[there, to] = zsum[first : first + 16, :].astype(BF16)
+    for q in (6, 2, 5, 3, 4, 7, 1, 0):
+        for to in (core, 1 - core)[q == 0 :]:
+            send(
+                win_out.at[(plane + q) % 8, to],
+                win_in.at[core, q],
+                win_ss.at[to, q],
+                win_rs.at[core, q],
+                in_plane(q, to),
+            )
+    win_in[core, 0] = win_out[plane, core]
 
     total = xsum[rows(zpos * ZWIN, ZWIN), :]
     for q in range(1, 8):
         arrived(zwin_in.at[q - 1], zwin_ss.at[q - 1], zwin_rs.at[q - 1])
         total = total + zwin_in[q - 1].astype(F32)
 
-    def turned(value, start):
-        size = value.shape[0]
-        return pltpu.roll(value, (size - start) % size, 0)
-
-    lower, upper = total[0:HWIN, :], total[HWIN:, :]
-    y_out[...] = jnp.concatenate(
-        [jnp.where(half == 0, upper, lower), jnp.zeros((WIN - HWIN, CX), F32)], axis=0
-    ).astype(BF16)
-    send(y_out, y_in, y_ss, y_rs, in_plane(4))
-    mine_x = jnp.where(half == 0, lower, upper)
+    parts[0:ZWIN, :] = pltpu.roll(total, (ZWIN - 2 * xpos) % ZWIN, 0)
+    parts[ZWIN:, :] = jnp.zeros((16, CX), F32)
+    for to_half in range(2):
+        for to in range(2):
+            first = HWIN * to_half + OUT * to
+            y_out[to_half, to] = parts[first : first + 16, :].astype(BF16)
+    for other, to in ((1, core), (1, 1 - core), (0, 1 - core)):
+        send(
+            y_out.at[(half + other) % 2, to],
+            y_in.at[core, other],
+            y_ss.at[to, other],
+            y_rs.at[core, other],
+            in_plane(4 * other, to),
+        )
+    y_in[core, 0] = y_out[half, core]
 
     arrived(gt_in, pair_ss.at[2], pair_rs.at[2])
     gtxt[...] = gt_out[...].astype(F32) + gt_in[...].astype(F32)
     arrived(gi_in, pair_ss.at[4], pair_rs.at[4])
     gimg[...] = gimg[...] + gi_in[...].astype(F32)
-
-    total = zsum[rows(plane * 16, WIN), :]
-    for q in range(1, 8):
-        arrived(win_in.at[q - 1], win_ss.at[q - 1], win_rs.at[q - 1])
-        total = total + win_in[q - 1].astype(F32)
-    mine_z = turned(total, 2 * plane)
-    arrived(y_in, y_ss, y_rs)
-    mine_x = turned(mine_x + y_in[...].astype(F32)[0:HWIN, :], 2 * xpos)
-    fin_out[:, 0:CZ] = turned(mine_z, OUT * (1 - core))[0:16, :]
-    fin_out[:, CZ:] = turned(mine_x, OUT * (1 - core))[0:16, :]
-    send(fin_out, fin_in, fin_ss, fin_rs, (sibling, mp))
-    keep = jnp.concatenate(
-        [turned(mine_z, OUT * core)[0:OUT, :], turned(mine_x, OUT * core)[0:OUT, :]], axis=1
-    )
-    arrived(fin_in, fin_ss, fin_rs)
-    other = fin_in[0:OUT, :]
-    gup[...] = jnp.where(core == 0, keep, other)
-    gdn[...] = jnp.where(core == 0, other, keep)
+    stores.append(load(gtxt, gtxt_h, 7))
+    stores.append(load(gimg, gimg_h, 8))
+
+    arrived(win_in.at[1 - core, 0], win_ss.at[1 - core, 0], win_rs.at[1 - core, 0])
+    arrived(y_in.at[1 - core, 0], y_ss.at[1 - core, 0], y_rs.at[1 - core, 0])
+    for origin, result in ((0, gup), (1, gdn)):
+        total = win_in[origin, 0].astype(F32)
+        for q in range(1, 8):
+            arrived(win_in.at[origin, q], win_ss.at[origin, q], win_rs.at[origin, q])
+            total = total + win_in[origin, q].astype(F32)
+        result[:, 0:CZ] = total[0:OUT, :]
+    for origin, result in ((0, gup), (1, gdn)):
+        arrived(y_in.at[origin, 1], y_ss.at[origin, 1], y_rs.at[origin, 1])
+        total = y_in[origin, 0].astype(F32) + y_in[origin, 1].astype(F32)
+        result[:, CZ:] = total[0:OUT, :]
+    stores.append(load(gup, gup_h, 9))
+    stores.append(load(gdn, gdn_h, 10))
+    for store in stores:
+        store.wait()
 
     for copy in pending:
         copy.wait_send()
@@ -601,8 +623,13 @@
             jax.ShapeDtypeStruct((TOK, D), BF16),
         ),
         in_specs=[smem, smem, hbm, hbm, vmem, vmem, hbm, hbm, hbm, hbm],
-        out_specs=(vmem, vmem, vmem, vmem, vmem),
+        out_specs=(hbm, hbm, hbm, hbm, hbm),
         scratch_shapes=[
+            pltpu.VMEM((IMGS, D), F32),
+            pltpu.VMEM((TXTS, D), F32),
+            pltpu.VMEM((OUT, HALF), F32),
+            pltpu.VMEM((OUT, HALF), F32),
+            pltpu.VMEM((TOK, D), BF16),
             pltpu.VMEM((IMGS, D + META), BF16),
             pltpu.VMEM((TXTS, D), BF16),
             pltpu.VMEM((TOK, D), BF16),
@@ -627,16 +654,15 @@
             pltpu.VMEM((2, XROWS, CX), BF16),
             pltpu.VMEM((2, XROWS, CX), BF16),
             pltpu.VMEM((2, XROWS, CX), BF16),
-            pltpu.VMEM((ZROWS, CZ), F32),
-            pltpu.VMEM((ZROWS, CZ), BF16),
+            pltpu.VMEM((ZROWS + 16, CZ), F32),
             pltpu.VMEM((XROWS, CX), F32),
             pltpu.VMEM((XROWS, CX), BF16),
-            pltpu.VMEM((7, WIN, CZ), BF16),
+            pltpu.VMEM((8, 2, 16, CZ), BF16),
+            pltpu.VMEM((2, 8, 16, CZ), BF16),
             pltpu.VMEM((7, ZWIN, CX), BF16),
-            pltpu.VMEM((WIN, CX), BF16),
-            pltpu.VMEM((WIN, CX), BF16),
-            pltpu.VMEM((16, HALF), F32),
-            pltpu.VMEM((16, HALF), F32),
+            pltpu.VMEM((2, 2, 16, CX), BF16),
+            pltpu.VMEM((2, 2, 16, CX), BF16),
+            pltpu.VMEM((ZWIN + 16, CX), F32),
             pltpu.VMEM((TXTS, D), BF16),
             pltpu.VMEM((STEPS, HTXT, D), BF16),
             pltpu.VMEM((STEPS, IMGS, D + META), BF16),
@@ -650,7 +676,7 @@
             pltpu.VMEM((TXTS, D), BF16),
             pltpu.VMEM((IMGS, D), BF16),
             pltpu.VMEM((IMGS, D), BF16),
-            dma((6,)),
+            dma((11,)),
             dma((7,)),
             dma((7,)),
             dma((7,)),
@@ -667,14 +693,12 @@
             dma((2, NXSUB)),
             dma((2, NXSUB)),
             dma((2, NXSUB)),
+            dma((2, 8)),
+            dma((2, 8)),
             dma((7,)),
             dma((7,)),
-            dma((7,)),
-            dma((7,)),
-            dma,
-            dma,
-            dma,
-            dma,
+            dma((2, 2)),
+            dma((2, 2)),
         ],
         compiler_params=pltpu.CompilerParams(
             collective_id=0, has_side_effects=True, vmem_limit_bytes=58 * 1024 * 1024

time: 65 us -> 62.6 us (0.963)
  Pallas kernels: 62.9 us -> 60.2 us
    pallas_call x1, Pallas kernels: 60.2 us -> 57.4 us  [shards(): pl.pallas_call(step_kernel, out_shape=(jax.ShapeDtypeStruct((IMGS, D), F3...]
where the time goes in v4:
time: 62.6 us; the launch traced here: 62.1 us
  Pallas kernels  60.2 us (96%)
  between operations  1.93 us (3%)
    pallas_call x1, Pallas kernels, shards(): pl.pallas_call(step_kernel, out_shape=(jax.ShapeDtypeStruct((IMGS, D), F3...  57.4 us
    pallas_call x1, Pallas kernels, shards(): pl.pallas_call(hand_over, out_shape=tuple((jax.ShapeDtypeStruct(x.shape,...  2.78 us

profile of v4, /device:TPU:1, one launch (start us, length us, event | category | flops | bytes accessed | tf_op | source)
XLA Modules:
  0.0 62.1 jit_solution(3188992290112498965)
XLA Ops:
  1.9 57.4 %step.1 = (f32[64,1152]{1,0:T(8,128)}, f32[128,1152]{1,0:T(8,128)}, f32[9,1152]{1,0:T(8,128)}, f32[9,1152]{1,0:T(8,128)}, bf16[384,1152]{1,0:T(8,128)(2,1)}) custom-call(f32[1]{0:T(128)S(6)} %copy.15.scale_ref, f32[1]{0:T(128)S(6)} %copy.16.bias_ref, bf16[64,1152]{1,0:T(8,128)(2,1)} %img_h.1, bf16[128,1152]{1,0:T(8,128)(2,1)} %txt_h.1, s32[1,64]{1,0:T(1,128)} %bitcast.2, ...), custom_call_target="tpu_custom_call" | custom-call | tf_op jit(solution)/shard_map/step/pallas_call | solution.py:616
  59.3 2.8 %hand_over.1 = (f32[64,1152]{1,0:T(8,128)}, f32[128,1152]{1,0:T(8,128)}, f32[9,1152]{1,0:T(8,128)}, f32[9,1152]{1,0:T(8,128)}, bf16[384,1152]{1,0:T(8,128)(2,1)}) custom-call(f32[64,1152]{1,0:T(8,128)} %get-tuple-element.10.refs_0_, f32[128,1152]{1,0:T(8,128)} %get-tuple-element.11.refs_1_, f32[9,1152]{1,0:T(8,128)} %get-tuple-element.12.refs_2_, ...), custom_call_target="tpu_custom_call" | custom-call | tf_op jit(solution)/shard_map/hand_over/pallas_call | solution.py:708

commit v5 on v4

--- a/solution.py
+++ b/solution.py
@@ -466,22 +466,22 @@
 
     z_step(3)
 
-    for c in range(NXSUB):
-        part = pl.ds(c * XSUB, XSUB)
+    for turn in (2, 1, 3, 0):
+        c = (zpos // 2 + turn) % NXSUB
+        part = rows(c * XSUB, XSUB)
         arrived(xd_in.at[1, part], xd_ss.at[1, c], xd_rs.at[1, c])
         arrived(xu_in.at[1, part], xu_ss.at[1, c], xu_rs.at[1, c])
         value = x_term(0, c) + xd_in[1, part, :].astype(F32) + xu_in[1, part, :].astype(F32)
         xsum[part, :] = value
         xsum_bf[part, :] = value.astype(BF16)
-
-    for q in (4, 3, 5, 2, 6, 1, 7):
-        send(
-            xsum_bf.at[rows((zpos + q) % NZ * ZWIN, ZWIN)],
-            zwin_in.at[q - 1],
-            zwin_ss.at[q - 1],
-            zwin_rs.at[q - 1],
-            along_z(q),
-        )
+        for there in ((2 * c, 2 * c + 1) if turn else (zpos + 1 - 2 * (zpos % 2),)):
+            send(
+                xsum_bf.at[rows(there * ZWIN, ZWIN)],
+                zwin_in.at[zpos],
+                zwin_ss.at[there],
+                zwin_rs.at[zpos],
+                along_z((there - zpos + NZ) % NZ),
+            )
 
     arrived(img_too, pair_ss.at[3], pair_rs.at[3])
     full = img_too[:, 0:D].astype(F32)
@@ -552,8 +552,9 @@
 
     total = xsum[rows(zpos * ZWIN, ZWIN), :]
     for q in range(1, 8):
-        arrived(zwin_in.at[q - 1], zwin_ss.at[q - 1], zwin_rs.at[q - 1])
-        total = total + zwin_in[q - 1].astype(F32)
+        there = (zpos + q) % NZ
+        arrived(zwin_in.at[there], zwin_ss.at[there], zwin_rs.at[there])
+        total = total + zwin_in[there].astype(F32)
 
     parts[0:ZWIN, :] = pltpu.roll(total, (ZWIN - 2 * xpos) % ZWIN, 0)
     parts[ZWIN:, :] = jnp.zeros((16, CX), F32)
@@ -600,8 +601,17 @@
 
 
 def hand_over(*refs):
-    for i in range(5):
-        refs[5 + i][...] = refs[i][...]
+    sources, targets, held, sems = refs[0:5], refs[5:10], refs[10:15], refs[15]
+    order = (4, 1, 0, 2, 3)
+    into = [pltpu.make_async_copy(sources[i], held[i], sems.at[0, i]) for i in order]
+    onto = [pltpu.make_async_copy(held[i], targets[i], sems.at[1, i]) for i in order]
+    for copy in into:
+        copy.start()
+    for copy, after in zip(into, onto):
+        copy.wait()
+        after.start()
+    for after in onto:
+        after.wait()
 
 
 def shards(
@@ -659,7 +669,7 @@
             pltpu.VMEM((XROWS, CX), BF16),
             pltpu.VMEM((8, 2, 16, CZ), BF16),
             pltpu.VMEM((2, 8, 16, CZ), BF16),
-            pltpu.VMEM((7, ZWIN, CX), BF16),
+            pltpu.VMEM((NZ, ZWIN, CX), BF16),
             pltpu.VMEM((2, 2, 16, CX), BF16),
             pltpu.VMEM((2, 2, 16, CX), BF16),
             pltpu.VMEM((ZWIN + 16, CX), F32),
@@ -695,8 +705,8 @@
             dma((2, NXSUB)),
             dma((2, 8)),
             dma((2, 8)),
-            dma((7,)),
-            dma((7,)),
+            dma((NZ,)),
+            dma((NZ,)),
             dma((2, 2)),
             dma((2, 2)),
         ],
@@ -708,8 +718,9 @@
     return pl.pallas_call(
         hand_over,
         out_shape=tuple(jax.ShapeDtypeStruct(x.shape, x.dtype) for x in out),
-        in_specs=[vmem] * 5,
-        out_specs=(vmem,) * 5,
+        in_specs=[hbm] * 5,
+        out_specs=(hbm,) * 5,
+        scratch_shapes=[pltpu.VMEM(x.shape, x.dtype) for x in out] + [dma((2, 5))],
         name="hand_over",
     )(*out)
 

time: 62.6 us -> 62.3 us (level)
  no operation moved by 1% of the time
where the time goes in v5:
time: 62.3 us; the launch traced here: 62.2 us
  Pallas kernels  60.2 us (97%)
  between operations  1.93 us (3%)
    pallas_call x1, Pallas kernels, shards(): pl.pallas_call(step_kernel, out_shape=(jax.ShapeDtypeStruct((IMGS, D), F3...  57.7 us
    pallas_call x1, Pallas kernels, shards(): pl.pallas_call(hand_over, out_shape=tuple((jax.ShapeDtypeStruct(x.shape,...  2.5 us

profile of v5, /device:TPU:1, one launch (start us, length us, event | category | flops | bytes accessed | tf_op | source)
XLA Modules:
  0.0 62.2 jit_solution(13438262053254981388)
XLA Ops:
  1.9 57.7 %step.1 = (f32[64,1152]{1,0:T(8,128)}, f32[128,1152]{1,0:T(8,128)}, f32[9,1152]{1,0:T(8,128)}, f32[9,1152]{1,0:T(8,128)}, bf16[384,1152]{1,0:T(8,128)(2,1)}) custom-call(f32[1]{0:T(128)S(6)} %copy.15.scale_ref, f32[1]{0:T(128)S(6)} %copy.16.bias_ref, bf16[64,1152]{1,0:T(8,128)(2,1)} %img_h.1, bf16[128,1152]{1,0:T(8,128)(2,1)} %txt_h.1, s32[1,64]{1,0:T(1,128)} %bitcast.2, ...), custom_call_target="tpu_custom_call" | custom-call | tf_op jit(solution)/shard_map/step/pallas_call | solution.py:626
  59.7 2.5 %hand_over.1 = (f32[64,1152]{1,0:T(8,128)}, f32[128,1152]{1,0:T(8,128)}, f32[9,1152]{1,0:T(8,128)}, f32[9,1152]{1,0:T(8,128)}, bf16[384,1152]{1,0:T(8,128)(2,1)}) custom-call(f32[64,1152]{1,0:T(8,128)} %get-tuple-element.10.refs_0_, f32[128,1152]{1,0:T(8,128)} %get-tuple-element.11.refs_1_, f32[9,1152]{1,0:T(8,128)} %get-tuple-element.12.refs_2_, ...), custom_call_target="tpu_custom_call" | custom-call | tf_op jit(solution)/shard_map/hand_over/pallas_call | solution.py:718
